TPU v7x, 32 devices: a whole 2x2x4 slice. The times are simulated.
32 devices in a mesh: dp: 16 (over z, x, core), band: 2 (over y).
Axes of the slice: x: 2, y: 2, z: 4, core: 2. Of those that a mesh axis runs over, the one named last changes fastest.
Arguments:
- pixels: bfloat16 [384, 10, 256, 64], P('dp', 'band'), may hold values from -6 to 6
- visible: int32 [384, 64], P('dp'), may hold values from 0 to 255, as said below
- kernels: bfloat16 [10, 64, 768], P('band'), may hold values from -0.25 to 0.25
- class_token: float32 [768], replicated, may hold values from -5 to 5
- norm1_gain: float32 [768], replicated, may hold values from 0.1 to 1.9
- norm1_bias: float32 [768], replicated, may hold values from -3 to 3
- norm2_gain: float32 [768], replicated, may hold values from 0.1 to 1.9
- norm2_bias: float32 [768], replicated, may hold values from -3 to 3
- attn_qkv: bfloat16 [768, 2304], replicated, may hold values from -0.21875 to 0.21875
- attn_out: bfloat16 [768, 768], replicated, may hold values from -0.4375 to 0.4375
- mlp_up: bfloat16 [768, 3072], replicated, may hold values from -0.21875 to 0.21875
- mlp_down: bfloat16 [3072, 768], replicated, may hold values from -0.109375 to 0.109375
- cotangent: bfloat16 [384, 65, 768], P(('dp', 'band')), may hold values from -6 to 6
Outputs:
- block_output: bfloat16 [384, 65, 768], P(('dp', 'band'))
- pixel_grads: float32 [384, 10, 256, 64], P('dp', 'band')
- kernel_grads: float32 [10, 64, 768], P('band')
- class_grad: float32 [768], replicated
- norm1_gain_grad: float32 [768], replicated
- norm1_bias_grad: float32 [768], replicated
- norm2_gain_grad: float32 [768], replicated
- norm2_bias_grad: float32 [768], replicated
- qkv_grad: float32 [768, 2304], P('band', 'dp')
- outproj_grad: float32 [768, 768], P('band', 'dp')
- up_grad: float32 [768, 3072], P('band', 'dp')
- down_grad: float32 [3072, 768], P('band', 'dp')
Inputs may be any that keep to these rules, and one draw needn't show every extreme that they name: `visible`: each row holds 64 different patch numbers, in no particular order.
All inputs are finite; a program needn't handle non-finite values.
Results may differ from a plain program's by a relative error of at most 0.015.
Values may be sent and summed in bfloat16 or wider, within the bound.
No kernel may reach another device: no remote copies, remote signals or barrier semaphores. Data moves between devices by JAX's collectives and lax.ppermute only.
A program may use at most 192 MiB of HBM per device.

v0:
```python
import functools

import jax
import jax.numpy as jnp
from jax import lax
from jax.experimental import pallas as pl
from jax.experimental.pallas import tpu as pltpu
from jax.sharding import PartitionSpec as P

HEADS = 12
HEAD = 64
BF = jnp.bfloat16
F32 = jnp.float32
TAIL = 16
BLOCK = 112
KEYS = 80
SCALE = HEAD ** (-0.5)
VMEM = pl.BlockSpec(memory_space=pltpu.VMEM)
HBM = pl.BlockSpec(memory_space=pl.ANY)
shape = jax.ShapeDtypeStruct
MICROSECONDS = {
    "pick_far": 5,
    "prepare": 11,
    "encoder_forward": 31,
    "mlp_back": 32,
    "attention_back": 18,
    "embed_back": 14,
    "combine": 12,
    "touch": 20,
    "assemble": 0.5,
    "finish": 0.5,
    "scatter": 4,
}


def dot(a, b):
    return jnp.dot(a, b, preferred_element_type=F32)


def dot_nt(a, b):
    return lax.dot_general(a, b, (((1,), (1,)), ((), ())), preferred_element_type=F32)


def dot_tn(a, b):
    return lax.dot_general(a, b, (((0,), (0,)), ((), ())), preferred_element_type=F32)


def kernel_call(body, name, outs, scratch, copies, vmem_in=0, vmem_out=0, mib=62, **more):
    def call(*operands):
        return pl.pallas_call(
            body,
            out_shape=tuple(outs),
            in_specs=[VMEM] * vmem_in + [HBM] * (len(operands) - vmem_in),
            out_specs=(HBM,) * (len(outs) - vmem_out) + (VMEM,) * vmem_out,
            scratch_shapes=[
                a if hasattr(a, "get_ref_aval") else pltpu.VMEM(a.shape, a.dtype) for a in scratch
            ]
            + [pltpu.SemaphoreType.DMA((copies,))],
            compiler_params=pltpu.CompilerParams(vmem_limit_bytes=mib * 1024 * 1024),
            cost_estimate=pl.CostEstimate(
                flops=int(MICROSECONDS[name] * 1.15e9), bytes_accessed=1, transcendentals=0
            ),
            name=name,
            **more,
        )(*operands)

    return call


def tiles(count, body, looped=False, base=0, tile=256):
    if not looped:
        for j in range(0, count, tile):
            body(slice(base + j, base + j + tile))
        return

    def step(j, carry):
        body(pl.ds(pl.multiple_of(base + j * tile, tile), tile))
        return carry

    lax.fori_loop(0, count // tile, step, 0)


LOOP = (True, False, True, True, False)


class Copies:
    def __init__(self, sems):
        self.sems, self.count, self.open = sems, 0, []

    def start(self, source, target):
        copy = pltpu.make_async_copy(source, target, self.sems.at[self.count])
        self.count += 1
        copy.start()
        return copy

    def out(self, source, target):
        self.open.append(self.start(source, target))

    def finish(self):
        for copy in self.open:
            copy.wait()


def chosen(seen_ref, chip, patches):
    first = seen_ref[pl.ds(chip, 1), :]
    second = seen_ref[pl.ds(chip + 1, 1), :]
    slots = first.shape[1]
    seen = jnp.concatenate([first, second], axis=1)
    ids = lax.broadcasted_iota(jnp.int32, (patches, 2 * slots), 0)
    lane = lax.broadcasted_iota(jnp.int32, (patches, 2 * slots), 1)
    hit = ids == seen
    return (
        jnp.where(hit & (lane < slots), 1.0, 0.0).astype(BF),
        jnp.where(hit & (lane >= slots), 1.0, 0.0).astype(BF),
    )


class Pixels:
    def __init__(self, pixel_hbm, pixel_ref, base, pairs, sems):
        self.hbm, self.ref, self.base, self.pairs, self.sems = pixel_hbm, pixel_ref, base, pairs, sems
        for i in range(pairs):
            self.copy(i).start()

    def copy(self, i):
        there, here = pl.ds(self.base + 2 * i, 2), pl.ds(2 * i, 2)
        return pltpu.make_async_copy(self.hbm.at[there], self.ref.at[here], self.sems.at[i])

    def pick(self, seen_ref, out_ref):
        wide = 2 * seen_ref.shape[1]

        def pair(i, carry):
            first, second = chosen(seen_ref, self.base + 2 * i, self.ref.shape[2])
            self.copy(i).wait()
            out_ref[:, pl.ds(pl.multiple_of(i * wide, wide), wide)] = (
                dot(self.ref[2 * i], first) + dot(self.ref[2 * i + 1], second)
            ).astype(BF)
            return carry

        lax.fori_loop(0, self.pairs, pair, 0)


def pick_far_kernel(
    links, pairs, seen_ref, pixel_hbm, halves_hbm, half_hbm, out_hbm, pixel_ref, out_ref, half_ref, pixel_sems, sems
):
    copies = Copies(sems)
    base = (1 - links.bit("band")) * 2 * pairs
    half_in = copies.start(halves_hbm.at[links.bit(0)], half_ref)
    pixels = Pixels(pixel_hbm, pixel_ref, base, pairs, pixel_sems)
    half_in.wait()
    copies.out(half_ref, half_hbm)
    pixels.pick(seen_ref, out_ref)
    copies.out(out_ref, out_hbm)
    copies.finish()


def pick_far(links, seen, pixel_rows, halves):
    chips, depth, patches = pixel_rows.shape
    pairs = chips // 4
    outs = (shape(halves.shape[1:], BF), shape((depth, chips // 2 * seen.shape[1]), BF))
    return kernel_call(
        functools.partial(pick_far_kernel, links, pairs),
        "pick_far",
        outs,
        (
            shape((2 * pairs, depth, patches), BF),
            outs[1],
            outs[0],
            pltpu.SemaphoreType.DMA((pairs,)),
        ),
        4,
        vmem_in=1,
    )(seen, pixel_rows, halves)


def prepare_kernel(
    links,
    pairs,
    seen_ref,
    pixel_hbm,
    cot_hbm,
    down_hbm,
    picked_hbm,
    rows_hbm,
    gact_hbm,
    pixel_ref,
    cot_ref,
    down_ref,
    picked_ref,
    rows_ref,
    gact_ref,
    tail_ref,
    pixel_sems,
    sems,
):
    copies = Copies(sems)
    chips = cot_ref.shape[0]
    slots = cot_ref.shape[1] - 1
    rows, width = rows_ref.shape
    base = links.bit("band") * 2 * pairs
    cot_in = copies.start(cot_hbm, cot_ref)
    pixels = Pixels(pixel_hbm, pixel_ref, base, pairs, pixel_sems)
    chunk = down_hbm.shape[0] // 4
    parts = [slice(i * chunk, (i + 1) * chunk) for i in range(4)]
    downs = [copies.start(down_hbm.at[part, :], down_ref.at[part, :]) for part in parts]
    cot_in.wait()
    tail_ref[...] = jnp.zeros_like(tail_ref)

    def lay(c, carry):
        chip = cot_ref[c].astype(F32)
        rows_ref[pl.ds(pl.multiple_of(c * slots, slots), slots), :] = chip[1:, :].astype(BF)
        tail_ref[pl.ds(c, 1), :] = chip[0:1, :]
        return carry

    lax.fori_loop(0, chips, lay, 0)
    rows_ref[rows - TAIL : rows, :] = tail_ref[...].astype(BF)
    copies.out(rows_ref, rows_hbm)
    pixels.pick(seen_ref, picked_ref)
    copies.out(picked_ref, picked_hbm)
    for part, copy in zip(parts, downs):
        copy.wait()

        def act_grad(at):
            gact_ref[:, at] = dot_nt(rows_ref[...], down_ref[at, :]).astype(BF)

        tiles(chunk, act_grad, True, part.start)
        copies.out(gact_ref.at[:, part], gact_hbm.at[:, part])
    copies.finish()


def prepare(links, seen, pixel_rows, cot, down):
    group, depth, patches = pixel_rows.shape
    pairs = group // 4
    hidden, width = down.shape
    body = cot.shape[0] * seen.shape[1]
    rows = body + TAIL
    outs = (shape((depth, body), BF), shape((rows, width), BF), shape((rows, hidden), BF))
    return kernel_call(
        functools.partial(prepare_kernel, links, pairs),
        "prepare",
        outs,
        (shape((2 * pairs, depth, patches), BF), cot, down)
        + outs
        + (shape((TAIL, width), F32), pltpu.SemaphoreType.DMA((pairs,))),
        12,
        vmem_in=1,
    )(seen, pixel_rows, cot, down)


def row_stats(values):
    average = jnp.mean(values, axis=-1, keepdims=True)
    centred = values - average
    spread = jnp.mean(centred * centred, axis=-1, keepdims=True)
    root = lax.rsqrt(spread + 1e-06)
    return centred * root, root


def norm_back(xhat, root, grad_out, gain):
    scaled = grad_out * gain
    mean_scaled = jnp.mean(scaled, axis=-1, keepdims=True)
    mean_along = jnp.mean(scaled * xhat, axis=-1, keepdims=True)
    return root * (scaled - mean_scaled - xhat * mean_along)


def head_rows(width):
    row = lax.broadcasted_iota(jnp.int32, (TAIL, width), 0)
    lane = lax.broadcasted_iota(jnp.int32, (TAIL, width), 1)
    return (lane // HEAD) == row


def two_heads(pair):
    low = lax.broadcasted_iota(jnp.int32, pair.shape, 1) < HEAD
    zero = jnp.zeros_like(pair)
    return jnp.concatenate([jnp.where(low, pair, zero), jnp.where(low, zero, pair)], axis=0)


def own_heads(stacked):
    rows = stacked.shape[0] // 2
    low = lax.broadcasted_iota(jnp.int32, (rows, stacked.shape[1]), 1) < HEAD
    return jnp.where(low, stacked[:rows], stacked[rows:])


def softmax_keys(scores, count):
    key = lax.broadcasted_iota(jnp.int32, scores.shape, 0)
    scores = jnp.where(key < count, scores * SCALE, -1e30)
    raised = jnp.exp(scores - jnp.max(scores, axis=0, keepdims=True))
    return raised * (1.0 / jnp.sum(raised, axis=0, keepdims=True))


def load_far(links, copies, half_hbm, other_hbm, target):
    count = half_hbm.shape[0]
    core = links.bit(0)
    return [
        copies.start(half_hbm, target.at[pl.ds(pl.multiple_of(core * count, 16), count), :]),
        copies.start(other_hbm, target.at[pl.ds(pl.multiple_of((1 - core) * count, 16), count), :]),
    ]


def forward_kernel(
    links,
    chips,
    vecs_ref,
    xo_hbm,
    xr_hbm,
    ko_hbm,
    half_hbm,
    other_hbm,
    wqkv_hbm,
    wout_hbm,
    cot_hbm,
    gact_hbm,
    up_hbm,
    stream_hbm,
    n1_hbm,
    packed_hbm,
    probs_hbm,
    tprobs_hbm,
    att_hbm,
    mid_hbm,
    n2_hbm,
    act_hbm,
    gpre_hbm,
    down_send_hbm,
    down_keep_hbm,
    up_send_hbm,
    up_keep_hbm,
    stream_ref,
    n1_ref,
    packed_ref,
    probs_ref,
    tprobs_ref,
    att_ref,
    mid_ref,
    n2_ref,
    xo_ref,
    xr_ref,
    ko_ref,
    kr_ref,
    tatt_ref,
    wqkv_ref,
    wout_ref,
    *half_refs,
):
    copies = Copies(half_refs[-1])
    rows, width = n1_ref.shape
    body = rows - TAIL
    slots = body // chips
    token, gain1, bias1, gain2, bias2 = (vecs_ref[i : i + 1, :] for i in range(5))
    first = [
        copies.start(source, target)
        for source, target in ((xo_hbm, xo_ref), (ko_hbm, ko_ref), (xr_hbm, xr_ref))
    ] + load_far(links, copies, half_hbm, other_hbm, kr_ref)
    for copy in first:
        copy.wait()
    wqkv_in = copies.start(wqkv_hbm, wqkv_ref)
    wout_in = copies.start(wout_hbm, wout_ref)
    half = MlpHalf(links, 0, copies, half_refs[:-1])

    def embed(at):
        stream_ref[at, :] = dot_tn(xo_ref[:, at], ko_ref[...]) + dot_tn(xr_ref[:, at], kr_ref[...])

    tiles(body, embed, True)
    tail_row = lax.broadcasted_iota(jnp.int32, (TAIL, width), 0)
    stream_ref[body:rows, :] = jnp.where(tail_row < chips, token, 0.0)

    def first_norm(i, carry):
        at = pl.ds(pl.multiple_of(i * BLOCK, BLOCK), BLOCK)
        xhat, unused = row_stats(stream_ref[at, :])
        n1_ref[at, :] = (xhat * gain1 + bias1).astype(BF)
        return carry

    lax.fori_loop(0, rows // BLOCK, first_norm, 0)
    wqkv_in.wait()
    half.load(cot_hbm, gact_hbm, up_hbm)
    copies.out(stream_ref, stream_hbm)
    copies.out(n1_ref, n1_hbm)


    def project(at):
        packed_ref[:, at] = dot(n1_ref[...], wqkv_ref[:, at]).astype(BF)

    tiles(3 * width, project, True)
    copies.out(packed_ref, packed_hbm)
    tail = packed_ref[body:rows, :]
    heads = head_rows(width)
    tquery = jnp.where(heads, jnp.broadcast_to(tail[0:1, 0:width], (TAIL, width)), 0).astype(BF)
    tatt_ref[...] = jnp.zeros_like(tatt_ref)

    def chip(c, carry):
        at = pl.ds(pl.multiple_of(c * slots, slots), slots)
        key = jnp.concatenate(
            [packed_ref[at, width : 2 * width], tail[:, width : 2 * width]], axis=0
        )
        val = jnp.concatenate([packed_ref[at, 2 * width :], tail[:, 2 * width :]], axis=0)
        tiles = [slice(128 * p, 128 * p + 128) for p in range(width // 128)]
        scores = [dot_nt(key[:, here], two_heads(packed_ref[at, here])) for here in tiles]
        scores.append(dot_nt(key, tquery))
        probs = [softmax_keys(s, slots + 1).astype(BF) for s in scores]
        mixed = [dot_tn(probs[p], val[:, tiles[p]]) for p in range(len(tiles))]
        mixed.append(dot_tn(probs[-1], val))
        for p in range(len(tiles)):
            probs_ref[c, p] = probs[p]
            att_ref[at, tiles[p]] = own_heads(mixed[p]).astype(BF)
        tprobs_ref[c] = probs[-1]
        tatt_ref[pl.ds(c, 1), :] = jnp.sum(jnp.where(heads, mixed[-1], 0.0), axis=0, keepdims=True)
        return carry

    lax.fori_loop(0, chips, chip, 0, unroll=2)
    att_ref[body:rows, :] = tatt_ref[...].astype(BF)
    copies.out(probs_ref, probs_hbm)
    copies.out(tprobs_ref, tprobs_hbm)
    copies.out(att_ref, att_hbm)
    wout_in.wait()


    def out_project(at):
        mid_ref[:, at] = stream_ref[:, at] + dot(att_ref[...], wout_ref[:, at])

    tiles(width, out_project, True)
    copies.out(mid_ref, mid_hbm)

    def second_norm(i, carry):
        at = pl.ds(pl.multiple_of(i * BLOCK, BLOCK), BLOCK)
        xhat, unused = row_stats(mid_ref[at, :])
        n2_ref[at, :] = (xhat * gain2 + bias2).astype(BF)
        return carry

    lax.fori_loop(0, rows // BLOCK, second_norm, 0)
    copies.out(n2_ref, n2_hbm)
    half.run(n2_ref, (down_send_hbm, down_keep_hbm), (up_send_hbm, up_keep_hbm))
    copies.out(half.act, act_hbm)
    copies.out(half.gpre, gpre_hbm)
    copies.finish()


class MlpHalf:
    def __init__(self, links, third, copies, refs):
        self.links, self.third, self.copies = links, third, copies
        self.looped = (True, False)
        self.cot, self.gact, self.up, self.act, self.gpre, self.grads = refs

    @staticmethod
    def scratch(rows, width, hidden):
        return (
            shape((rows, width), BF),
            shape((rows, hidden // 2), BF),
            shape((width, hidden // 2), BF),
            shape((rows, hidden // 2), BF),
            shape((rows, hidden // 2), BF),
            shape((4, max(width, hidden // 4), width), BF),
        )

    def load(self, cot_hbm, gact_hbm, up_hbm):
        chunk = up_hbm.shape[1] // 4
        start = self.copies.start
        far = lambda i: slice((2 * i + self.third) * chunk, (2 * i + self.third + 1) * chunk)
        near = lambda i: slice(i * chunk, (i + 1) * chunk)
        self.first = [
            (
                start(up_hbm.at[:, far(i)], self.up.at[:, near(i)]),
                start(gact_hbm.at[:, far(i)], self.gact.at[:, near(i)]),
            )
            for i in range(2)
        ]
        self.cot_in = start(cot_hbm, self.cot)

    def run(self, n2_ref, down_out, up_out, then=None):
        copies, links = self.copies, self.links
        rows, width = n2_ref.shape
        chunk = self.up.shape[1] // 2
        half = width // 2
        block = width // 16
        for i in range(2):
            for copy in self.first[i]:
                copy.wait()
            if i == 1 and then is not None:
                then()

            def activate(cols):
                pre = dot(n2_ref[...], self.up[:, cols])
                phi = 0.5 + 0.5 * lax.erf(pre * (0.5**0.5))
                bell = jnp.exp(-0.5 * pre * pre) * 0.3989422804014327
                self.act[:, cols] = (pre * phi).astype(BF)
                gact = self.gact[:, cols].astype(F32)
                self.gpre[:, cols] = (gact * (phi + pre * bell)).astype(BF)

            tiles(chunk, activate, self.looped[0], i * chunk)
        where = (1, "band") if self.third == 0 else (0, 0)
        bits = [links.bit(w) for w in where]
        self.cot_in.wait()
        for i in range(2):

            def down_rows(at):
                self.grads[i, at, :] = dot_tn(
                    self.cot[:, at], self.act[:, i * chunk : (i + 1) * chunk]
                ).astype(BF)

            tiles(width, down_rows, self.looped[1])
            for side, bit in ((0, 1 - bits[0]), (1, bits[0])):
                for other in range(2):
                    x, c = (bit, other) if where[0] == 1 else (other, bit)
                    for z in range(4):
                        at = pl.multiple_of(((z * 2 + x) * 2 + c) * block, 16)
                        for h in range(2):
                            to = (((other * 2 + i) * 2 + h) * 4 + z) * block
                            copies.out(
                                self.grads.at[i, pl.ds(at, block), h * half : (h + 1) * half],
                                down_out[side].at[to : to + block, :],
                            )
        part = chunk // 4
        for i in range(2):

            def up_rows(at):
                self.grads[2 + i, at, :] = dot_tn(
                    self.gpre.at[:, i * chunk : (i + 1) * chunk][:, at], n2_ref[...]
                ).astype(BF)

            tiles(chunk, up_rows, self.looped[1])
            for side, bit in ((0, 1 - bits[1]), (1, bits[1])):
                for x in range(2):
                    for other in range(2):
                        if where[1] == "band":
                            at = (2 * x + other) * part
                            cols = pl.ds(pl.multiple_of(bit * half, 128), half)
                        else:
                            at = pl.multiple_of((2 * x + bit) * part, 16)
                            cols = slice(other * half, (other + 1) * half)
                        to = ((i * 2 + x) * 2 + other) * part
                        copies.out(
                            self.grads.at[2 + i, pl.ds(at, part), cols],
                            up_out[side].at[to : to + part, :],
                        )


def forward(links, chips, vecs, xo, xr, ko, half, other, wqkv, wout, cot, gact, up):
    width, hidden = up.shape
    body = xo.shape[1]
    rows = body + TAIL
    saved = (
        shape((rows, width), F32),
        shape((rows, width), BF),
        shape((rows, 3 * width), BF),
        shape((chips, width // 128, KEYS, 128), BF),
        shape((chips, KEYS, TAIL), BF),
        shape((rows, width), BF),
        shape((rows, width), F32),
        shape((rows, width), BF),
    )
    return kernel_call(
        functools.partial(forward_kernel, links, chips),
        "encoder_forward",
        saved
        + (shape((rows, hidden // 2), BF),) * 2
        + (shape((2 * width, width // 2), BF),) * 2
        + (shape((hidden // 2, width // 2), BF),) * 2,
        saved
        + (xo, xr, ko, ko, shape((TAIL, width), F32), wqkv, wout)
        + MlpHalf.scratch(rows, width, hidden),
        112,
        vmem_in=1,
    )(vecs, xo, xr, ko, half, other, wqkv, wout, cot, gact, up)


def spread_blocks(links, copies, full_ref, outs):
    core = links.bit(0)
    cols = full_ref.shape[1] // 2
    block = full_ref.shape[0] // 16
    for z in range(4):
        for x in range(2):
            for side, c in ((0, 1 - core), (1, core)):
                start = ((z * 2 + x) * 2 + c) * block
                for count, pair in outs:
                    rows = pl.ds(pl.multiple_of(start, 16), count)
                    start = start + count
                    for b in range(2):
                        to = ((x * 2 + b) * 4 + z) * count
                        copies.out(
                            full_ref.at[rows, b * cols : (b + 1) * cols],
                            pair[side].at[to : to + count, :],
                        )


def mlp_back_kernel(
    links,
    after,
    vecs_ref,
    n2_hbm,
    gact_hbm,
    act1_hbm,
    gpre1_hbm,
    up_hbm,
    down_hbm,
    mid_hbm,
    cot_hbm,
    att_hbm,
    wout_hbm,
    *rest,
):
    rest = rest[after:]
    sends, (keep_hbm, branch_hbm, gatt_hbm, out_hbm, vec_ref) = rest[:3], rest[3:8]
    (
        n2_ref,
        gatt_ref,
        out_ref,
        act_ref,
        gpre_ref,
        up_ref,
        down_ref,
        mid_ref,
        att_ref,
        wout_ref,
        back_ref,
        branch_ref,
        full_ref,
    ) = rest[8:21]
    half_refs, sems = rest[21:-1], rest[-1]
    copies = Copies(sems)
    rows, width = mid_ref.shape
    quarter = up_hbm.shape[1] // 4
    at = lambda i: slice(i * quarter, (i + 1) * quarter)
    n2_in = copies.start(n2_hbm, n2_ref)
    half = MlpHalf(links, 1, copies, half_refs)
    half.load(cot_hbm, gact_hbm, up_hbm)
    cot_ref = half.cot
    n2_in.wait()
    first_in = []

    def more():
        first_in.append(copies.start(gpre1_hbm, gpre_ref))
        for i in range(2):
            first_in.append(copies.start(up_hbm.at[:, at(2 * i)], up_ref.at[:, at(i)]))
        for source, target in ((mid_hbm, mid_ref), (att_hbm, att_ref), (wout_hbm, wout_ref)):
            first_in.append(copies.start(source, target))

    middle = 2 * width
    end = middle + up_hbm.shape[1] // 2
    half.run(
        n2_ref,
        (sends[0], keep_hbm.at[0:middle, :]),
        (sends[1], keep_hbm.at[middle:end, :]),
        more,
    )
    late = [copies.start(act1_hbm, act_ref)] + [
        copies.start(down_hbm.at[at(2 * i + third), :], down_ref.at[at(2 * third + i), :])
        for third in range(2)
        for i in range(2)
    ]
    for copy in first_in:
        copy.wait()

    def backward(cols):
        back_ref[:, cols] = dot_nt(gpre_ref[...], up_ref[cols, :]) + dot_nt(
            half.gpre[...], half.up[cols, :]
        )

    tiles(width, backward, LOOP[2])
    gain = vecs_ref[3:4, :]

    def norm(i, carry):
        at = pl.ds(pl.multiple_of(i * BLOCK, BLOCK), BLOCK)
        xhat, root = row_stats(mid_ref[at, :])
        grad = back_ref[at, :]
        total = cot_ref[at, :].astype(F32) + norm_back(xhat, root, grad, gain)
        branch_ref[at, :] = total.astype(BF)
        return (
            carry[0] + jnp.sum(grad * xhat, axis=0, keepdims=True),
            carry[1] + jnp.sum(grad, axis=0, keepdims=True),
        )

    zero = jnp.zeros((1, width), F32)
    gain_sum, bias_sum = lax.fori_loop(0, rows // BLOCK, norm, (zero, zero))
    vec_ref[0:1, :] = gain_sum
    vec_ref[1:2, :] = bias_sum
    copies.out(branch_ref, branch_hbm)

    def out_grad(at):
        full_ref[at, :] = dot_tn(branch_ref[:, at], att_ref[...]).astype(BF)

    tiles(width, out_grad, LOOP[4])
    spread_blocks(
        links, copies, full_ref, [(width // 16, (sends[2], keep_hbm.at[end : end + width, :]))]
    )

    def attended_grad(at):
        gatt_ref[:, at] = dot_nt(branch_ref[...], wout_ref[at, :]).astype(BF)

    tiles(width, attended_grad, LOOP[4])
    copies.out(gatt_ref, gatt_hbm)
    for copy in late:
        copy.wait()

    def outward(cols):
        out_ref[:, cols] = (
            mid_ref[:, cols]
            + dot(act_ref[...], down_ref[: 2 * quarter, cols])
            + dot(half.act[...], down_ref[2 * quarter :, cols])
        ).astype(BF)

    tiles(width, outward, LOOP[3])
    copies.out(out_ref, out_hbm)
    copies.finish()


def mlp_back(links, vecs, n2, gact, act1, gpre1, up, down, mid, cot, att, wout, after):
    rows, width = mid.shape
    hidden = up.shape[1]
    sums = shape((3 * width + hidden // 2, width // 2), BF)
    return kernel_call(
        functools.partial(mlp_back_kernel, links, len(after)),
        "mlp_back",
        tuple(shape((count, width // 2), BF) for count in (2 * width, hidden // 2, width))
        + (sums, cot, cot, cot, shape((2, width), F32)),
        (n2, cot, cot, act1, gpre1)
        + (shape((width, hidden // 2), BF), down, mid, att, wout, mid, cot, wout)
        + MlpHalf.scratch(rows, width, hidden),
        140,
        vmem_in=1,
        vmem_out=1,
    )(vecs, n2, gact, act1, gpre1, up, down, mid, cot, att, wout, *after)


def split_vec(vec):
    high = vec.astype(BF)
    return high, (vec - high.astype(F32)).astype(BF)


def attention_back_kernel(
    links, chips, after, gatt_hbm, packed_hbm, probs_hbm, tprobs_hbm, n1_hbm, *rest
):
    gpacked_hbm, send_hbm, keep_hbm = rest[after : after + 3]
    (
        gpacked_ref,
        gatt_ref,
        packed_ref,
        probs_ref,
        tprobs_ref,
        n1_ref,
        tgrad_ref,
        tout_ref,
        full_ref,
        chip_sems,
        sems,
    ) = rest[after + 3 :]
    rows, width = n1_ref.shape
    body = rows - TAIL
    slots = body // chips
    copies = Copies(sems)

    def arriving(c):
        at = pl.ds(pl.multiple_of(c * slots, slots), slots)
        return [
            pltpu.make_async_copy(source.at[where], target.at[where], chip_sems.at[k, c])
            for k, (source, target, where) in enumerate(
                (
                    (packed_hbm, packed_ref, (at, slice(None))),
                    (gatt_hbm, gatt_ref, (at, slice(None))),
                    (probs_hbm, probs_ref, c),
                )
            )
        ]

    tails = slice(body, rows)
    arrive = [
        copies.start(packed_hbm.at[tails, :], packed_ref.at[tails, :]),
        copies.start(gatt_hbm.at[tails, :], gatt_ref.at[tails, :]),
        copies.start(tprobs_hbm, tprobs_ref),
    ]
    for c in range(chips):
        for copy in arriving(c):
            copy.start()
    tout_ref[...] = jnp.zeros_like(tout_ref)
    heads = head_rows(width)
    for copy in arrive:
        copy.wait()
    n1_in = copies.start(n1_hbm, n1_ref)
    tgrad_ref[...] = gatt_ref[body:rows, :].astype(F32)
    tail = packed_ref[body:rows, :]
    tquery = jnp.where(heads, jnp.broadcast_to(tail[0:1, 0:width], (TAIL, width)), 0).astype(BF)

    def chip(c):
        at = pl.ds(pl.multiple_of(c * slots, slots), slots)
        key_all = jnp.concatenate(
            [packed_ref[at, width : 2 * width], tail[:, width : 2 * width]], axis=0
        )
        val_all = jnp.concatenate([packed_ref[at, 2 * width :], tail[:, 2 * width :]], axis=0)
        tgrad = jnp.where(
            heads, jnp.broadcast_to(tgrad_ref[pl.ds(c, 1), :], (TAIL, width)), 0.0
        ).astype(BF)
        tiles = [slice(128 * p, 128 * p + 128) for p in range(width // 128)]
        probs = [probs_ref[c, p] for p in range(len(tiles))] + [tprobs_ref[c]]
        gouts = [two_heads(gatt_ref[at, here]) for here in tiles]
        queries = [two_heads(packed_ref[at, here]) for here in tiles]
        gprobs = [dot_nt(val_all[:, tiles[p]], gouts[p]) for p in range(len(tiles))]
        gprobs.append(dot_nt(val_all, tgrad))
        gscores = []
        for prob, gprob in zip(probs, gprobs):
            wide = prob.astype(F32)
            inner = jnp.sum(gprob * wide, axis=0, keepdims=True)
            gscores.append((wide * (gprob - inner) * SCALE).astype(BF))
        gval_tail = dot(probs[-1], tgrad)
        gkey_tail = dot(gscores[-1], tquery)
        mixed = jnp.where(heads, dot_tn(gscores[-1], key_all), 0.0)
        gvals = [dot(probs[p], gouts[p]) + gval_tail[:, tiles[p]] for p in range(len(tiles))]
        gkeys = [dot(gscores[p], queries[p]) + gkey_tail[:, tiles[p]] for p in range(len(tiles))]
        gqueries = [own_heads(dot_tn(gscores[p], key_all[:, tiles[p]])) for p in range(len(tiles))]
        for p in range(len(tiles)):
            gpacked_ref[at, 128 * p : 128 * p + 128] = gqueries[p].astype(BF)
            base = width + 128 * p
            gpacked_ref[at, base : base + 128] = gkeys[p][:slots].astype(BF)
            gpacked_ref[at, width + base : width + base + 128] = gvals[p][:slots].astype(BF)
        tout_ref[pl.ds(c, 1), :] = jnp.concatenate(
            [jnp.sum(mixed, axis=0, keepdims=True)]
            + [g[slots : slots + 1] for g in gkeys + gvals],
            axis=1,
        )

    def two_chips(i, carry):
        for c in (2 * i, 2 * i + 1):
            for copy in arriving(c):
                copy.wait()
        chip(2 * i)
        chip(2 * i + 1)
        return carry

    lax.fori_loop(0, chips // 2, two_chips, 0)
    gpacked_ref[body:rows, :] = tout_ref[...].astype(BF)
    copies.out(gpacked_ref, gpacked_hbm)
    n1_in.wait()

    def qkv_rows(at):
        full_ref[at, :] = dot_tn(gpacked_ref[:, at], n1_ref[...]).astype(BF)

    tiles(3 * width, qkv_rows)
    outs = []
    for at, count in qkv_parts(width):
        here = slice(at, at + 16 * count)
        outs.append((count, (send_hbm.at[here, :], keep_hbm.at[here, :])))
    spread_blocks(links, copies, full_ref, outs)
    copies.finish()


def qkv_parts(width):
    block = 3 * width // 16
    count = -(-block // 32) * 16
    return [(0, count), (16 * count, block - count)]


def attention_back(links, chips, gatt, packed, probs, tprobs, n1, after):
    rows, width = n1.shape
    sums = shape((3 * width, width // 2), BF)
    return kernel_call(
        functools.partial(attention_back_kernel, links, chips, len(after)),
        "attention_back",
        (packed, sums, sums),
        (packed, gatt, packed, probs, tprobs, n1)
        + (
            shape((TAIL, width), F32),
            shape((TAIL, 3 * width), F32),
            shape((3 * width, width), BF),
            pltpu.SemaphoreType.DMA((3, chips)),
        ),
        80,
    )(gatt, packed, probs, tprobs, n1, *after)


def embed_back_kernel(
    links,
    chips,
    after,
    vecs_ref,
    vec2_ref,
    gpacked_hbm,
    wqkv_hbm,
    stream_hbm,
    branch_hbm,
    xo_hbm,
    xr_hbm,
    ko_hbm,
    half_hbm,
    other_hbm,
    *rest,
):
    send_hbm, keep_hbm, own_hbm, far_hbm, vec_ref = rest[after : after + 5]
    (
        gpacked_ref,
        wqkv_ref,
        stream_ref,
        branch_ref,
        xo_ref,
        xr_ref,
        ko_ref,
        kr_ref,
        send_ref,
        keep_ref,
        pgrad_ref,
        back_ref,
        embed_ref,
        kfull_ref,
        sems,
    ) = rest[after + 5 :]
    rows, width = stream_ref.shape
    body = rows - TAIL
    half = width // 2
    copies = Copies(sems)
    thirds = [slice(i * width, (i + 1) * width) for i in range(3)]
    arrive = [
        (
            copies.start(gpacked_hbm.at[:, part], gpacked_ref.at[:, part]),
            copies.start(wqkv_hbm.at[:, part], wqkv_ref.at[:, part]),
        )
        for part in thirds
    ]
    for i, part in enumerate(thirds):
        for copy in arrive[i]:
            copy.wait()
        if i == 0:
            late = [copies.start(stream_hbm, stream_ref), copies.start(branch_hbm, branch_ref)]
        if i == 1:
            last = [
                copies.start(source, target)
                for source, target in ((xo_hbm, xo_ref), (xr_hbm, xr_ref), (ko_hbm, ko_ref))
            ] + load_far(links, copies, half_hbm, other_hbm, kr_ref)

        def backward(cols):
            grad = dot_nt(gpacked_ref[:, part], wqkv_ref[cols, part])
            back_ref[:, cols] = grad if i == 0 else back_ref[:, cols] + grad

        tiles(width, backward, True)
    for copy in late:
        copy.wait()
    gain = vecs_ref[1:2, :]

    def norm(i, carry):
        at = pl.ds(pl.multiple_of(i * BLOCK, BLOCK), BLOCK)
        xhat, root = row_stats(stream_ref[at, :])
        grad = back_ref[at, :]
        total = branch_ref[at, :].astype(F32) + norm_back(xhat, root, grad, gain)
        back_ref[at, :] = total
        embed_ref[at, :] = total.astype(BF)
        return (
            carry[0] + jnp.sum(grad * xhat, axis=0, keepdims=True),
            carry[1] + jnp.sum(grad, axis=0, keepdims=True),
        )

    zero = jnp.zeros((1, width), F32)
    gain_sum, bias_sum = lax.fori_loop(0, rows // BLOCK, norm, (zero, zero))
    token_sum = jnp.sum(back_ref[body:rows, :], axis=0, keepdims=True)
    vec_ref[...] = jnp.zeros_like(vec_ref)
    for i, v in enumerate((gain_sum, bias_sum, token_sum, vec2_ref[0:1, :], vec2_ref[1:2, :])):
        vec_ref[2 * i : 2 * i + 1, :] = v[:, :half]
        vec_ref[2 * i + 1 : 2 * i + 2, :] = v[:, half:]
    for copy in last:
        copy.wait()
    grad = embed_ref[0:body, :]
    depth = xo_ref.shape[0]
    core, band = links.bit(0), links.bit("band")
    kfull_ref[0] = dot(xo_ref[...], grad).astype(BF)
    kfull_ref[1] = dot(xr_ref[...], grad).astype(BF)
    piece = depth // 4
    for c, ref in ((1 - core, send_ref), (core, keep_ref)):
        for far in range(2):
            for x in range(2):
                start = pl.multiple_of(c * (depth // 2) + x * piece, 16)
                block = kfull_ref[far, pl.ds(start, piece), :]
                for h in range(2):
                    slot = ((far + band - 2 * far * band) * 2 + x) * 2 + h
                    to = pl.ds(pl.multiple_of(slot * piece, 16), piece)
                    ref[to, :] = block[:, h * half : (h + 1) * half]
    high, low = split_vec(vec_ref[...])
    send_ref[2 * depth : 2 * depth + 16, :] = high
    send_ref[2 * depth + 16 : 2 * depth + 32, :] = low
    vec_ref[...] = high.astype(F32) + low.astype(F32)
    copies.out(send_ref, send_hbm)
    copies.out(keep_ref, keep_hbm)
    middle = body // 2
    for side, kernel, target in ((0, kr_ref, far_hbm), (1, ko_ref, own_hbm)):
        for h in range(2):
            part = grad[h * middle : (h + 1) * middle]
            pgrad_ref[side, h] = dot_nt(kernel[...], part).astype(BF)
        copies.out(pgrad_ref.at[side], target)
    copies.finish()


def embed_back(
    links, chips, vecs, vec2, gpacked, wqkv, stream, branch, xo, xr, ko, half, other, after
):
    rows, width = stream.shape
    depth, body = xo.shape
    cols = width // 2
    send, keep = shape((2 * depth + 32, cols), BF), shape((2 * depth, cols), BF)
    pgrad = shape((2, depth, body // 2), BF)
    return kernel_call(
        functools.partial(embed_back_kernel, links, chips, len(after)),
        "embed_back",
        (send, keep, pgrad, pgrad, shape((16, cols), F32)),
        (gpacked, wqkv, stream, branch, xo, xr, ko, ko, send, keep)
        + (
            shape((2,) + pgrad.shape, BF),
            stream,
            shape((rows, width), BF),
            shape((2, depth, width), BF),
        ),
        24,
        vmem_in=2,
        vmem_out=1,
    )(vecs, vec2, gpacked, wqkv, stream, branch, xo, xr, ko, half, other, *after)


def scatter_kernel(links, side, pairs, depth, seen_ref, grad_hbm, *rest):
    out_hbm, grad_ref, out_ref, sems = rest[-4:]
    patches = out_ref.shape[2]
    copies = Copies(sems)
    copies.start(grad_hbm.at[0 : 2 * depth, :], grad_ref).wait()
    band = links.bit("band")
    base = (band if side == 0 else 1 - band) * 2 * pairs
    wide = 2 * seen_ref.shape[1]
    half = grad_ref.shape[1] // wide

    def written(i):
        two = pl.ds(2 * i, 2)
        there = pl.ds(base + 2 * i, 2)
        return pltpu.make_async_copy(out_ref.at[two], out_hbm.at[there], sems.at[1 + i])

    def pair(i, carry):
        first, second = chosen(seen_ref, base + 2 * i, patches)
        row = pl.multiple_of(lax.div(i, half) * depth, 16)
        col = pl.multiple_of(lax.rem(i, half) * wide, 128)
        grad = grad_ref[pl.ds(row, depth), pl.ds(col, wide)]
        out_ref[2 * i] = dot_nt(grad, first)
        out_ref[2 * i + 1] = dot_nt(grad, second)
        written(i).start()
        return carry

    def landed(i, carry):
        written(i).wait()
        return carry

    lax.fori_loop(0, pairs, pair, 0)
    lax.fori_loop(0, pairs, landed, 0)


def scatter(links, side, grads, depth, seen, patches, *earlier):
    chips = seen.shape[0]
    pairs = chips // 4
    return kernel_call(
        functools.partial(scatter_kernel, links, side, pairs, depth),
        "scatter",
        (shape((chips, depth, patches), F32),),
        (shape((2 * depth, grads.shape[1]), BF), shape((2 * pairs, depth, patches), F32)),
        pairs + 1,
        vmem_in=1,
        input_output_aliases={2: 0} if earlier else {},
    )(seen, grads, *earlier)[0]


class Links:
    def __init__(self, mesh):
        self.count = mesh.shape["dp"]
        self.extra = self.count // 16

    def swap(self, array, *where):
        flip = sum((1 << w) * self.extra for w in where if w != "band")
        if "band" not in where:
            return lax.ppermute(array, "dp", [(d, d ^ flip) for d in range(self.count)])
        if flip == 0:
            return lax.ppermute(array, "band", [(0, 1), (1, 0)])
        pairs = [
            (2 * d + b, 2 * (d ^ flip) + 1 - b) for d in range(self.count) for b in range(2)
        ]
        return lax.ppermute(array, ("dp", "band"), pairs)

    def bring(self, array, *where):
        return pltpu.with_memory_space_constraint(self.swap(array, *where), pltpu.HBM)

    def bit(self, where):
        if where == "band":
            return lax.axis_index("band")
        return lax.rem(lax.div(lax.axis_index("dp"), self.extra << where), 2)

    def groups(self):
        return [[block * self.extra + i for i in range(self.extra)] for block in range(16)]

    def last(self, array):
        if self.extra == 1:
            return array
        return lax.psum_scatter(
            array, "dp", scatter_dimension=0, tiled=True, axis_index_groups=self.groups()
        )

    def total(self, array):
        if self.extra == 1:
            return array
        return lax.psum(array, "dp", axis_index_groups=self.groups())


class Level:
    def __init__(self, owner, terms, gone=frozenset(), rounded=False, alt=None, choice=None):
        self.owner, self.terms, self.gone, self.rounded = owner, list(terms), frozenset(gone), rounded
        self.alt, self.choice = alt, choice

    def moving(self, gone):
        strides = self.owner.strides(self.gone)
        return [(name, strides[name]) for name in self.owner.names if name in gone and name in strides]


class Piece:
    def __init__(self, names, sizes, unit, terms, gone=()):
        self.names, self.sizes, self.unit = list(names), list(sizes), unit
        self.gone = frozenset(gone)
        self.levels = [Level(self, terms, self.gone)]

    @staticmethod
    def join(first, second, choice):
        joined = Piece(first.names, first.sizes, first.unit, (), first.gone)
        joined.levels = [
            Level(a.owner, a.terms, a.gone, a.rounded, b, choice)
            for a, b in zip(first.levels, second.levels)
        ]
        return joined

    def strides(self, gone):
        found, stride = {}, self.unit
        for name, size in reversed(list(zip(self.names, self.sizes))):
            if name not in gone:
                found[name] = stride
                stride = stride * size
        return found

    def layout(self, names):
        gone = self.gone | frozenset(names)
        last = max([i for i, name in enumerate(self.names) if name in gone], default=-1)
        post = self.unit
        for size in self.sizes[last + 1 :]:
            post = post * size
        loops = [{}]
        for name, size in list(zip(self.names, self.sizes))[: last + 1]:
            if name not in gone:
                loops = [{**at, name: i} for at in loops for i in range(size)]
        return post * len(loops), post, loops


class Vec:
    def __init__(self, kept, came):
        self.kept, self.came = kept, [came]

    def value(self):
        parts = [
            buffer[at : at + 16].astype(F32) + buffer[at + 16 : at + 32].astype(F32)
            for buffer, at in self.came
        ]
        return pairwise([self.kept] + parts)


def pairwise(parts):
    while len(parts) > 1:
        parts = [
            parts[i] + parts[i + 1] if i + 1 < len(parts) else parts[i]
            for i in range(0, len(parts), 2)
        ]
    return parts[0]


def combine_kernel(links, tasks, n_in, n_out, n_load, after, *refs):
    ins, refs = refs[:n_in], refs[n_in + after :]
    out_hbm, refs = refs[:n_out], refs[n_out:]
    loads, refs = refs[:n_load], refs[n_load:]
    staged, sems = refs[:-1], refs[-1]
    copies = Copies(sems)
    bits = {where: links.bit(where) for where in (0, 1, 2, 3, "band")}
    waits = []
    for task in tasks:
        mine = []
        waits.append(mine)
        if task["kind"] == "raw":
            mine.append(copies.start(ins[task["from"]], loads[task["slot"]]))
            continue
        if task["kind"] == "vec":
            mine += [
                copies.start(ins[i].at[at : at + count, :], loads[slot])
                for i, at, count, slot in task["loads"]
            ]
            continue
        index = {
            name: (1 - bits[name]) if name in task["flip"] else bits[name] for name in bits
        }
        for load in task["loads"]:
            moving = sum((index[name] * stride for name, stride in load["moving"]), load["at"])
            alt_moving = sum(
                (index[name] * stride for name, stride in load["alt_moving"]), load["alt_at"]
            )
            for p, base in enumerate(load["bases"]):
                rows = pl.ds(pl.multiple_of(moving + base, 16), load["post"])
                target = loads[load["slot"]].at[p * load["post"] : (p + 1) * load["post"], :]
                sem = copies.sems.at[copies.count]
                copies.count += 1
                if load["alt"] is None:
                    copy = pltpu.make_async_copy(ins[load["in"]].at[rows, :], target, sem)
                    copy.start()
                else:
                    chosen_bit = index[load["choice"]]
                    copy = pltpu.make_async_copy(ins[load["in"]].at[rows, :], target, sem)
                    rows = pl.ds(pl.multiple_of(alt_moving + base, 16), load["post"])
                    other = pltpu.make_async_copy(ins[load["alt"]].at[rows, :], target, sem)
                    pl.when(chosen_bit == 0)(copy.start)
                    pl.when(chosen_bit == 1)(other.start)
                mine.append(copy)
    for task, mine in zip(tasks, waits):
        for copy in mine:
            copy.wait()
        if task["kind"] == "raw":
            copies.out(loads[task["slot"]], out_hbm[task["out"]].at[task["at"], :])
            continue
        if task["kind"] == "vec":
            parts = [loads[task["loads"][0][3]][...]]
            for unused, also, count, slot in task["loads"][1:]:
                parts.append(loads[slot][0:16, :].astype(F32) + loads[slot][16:32, :].astype(F32))
            high, low = split_vec(pairwise(parts))
            sent, kept = staged[task["stage"]], staged[task["stage"] + 1]
            sent[0:16, :] = high
            sent[16:32, :] = low
            kept[...] = high.astype(F32) + low.astype(F32)
            for out, at in task["outs"]:
                copies.out(sent, out_hbm[out].at[at, :])
            copies.out(kept, out_hbm[task["kept"]])
            continue
        result = staged[task["stage"]]
        count = result.shape[0]
        tile = max(t for t in (16, 32, 48, 64, 80, 96) if count % t == 0)

        def add(i, carry, task=task, result=result, tile=tile):
            at = pl.ds(pl.multiple_of(i * tile, 16), tile)
            total = None
            for rounded, slots in task["sum"]:
                parts = [loads[slot][at, :].astype(F32) for slot in slots]
                if total is not None:
                    parts = [total.astype(BF).astype(F32) if rounded else total] + parts
                total = pairwise(parts)
            result[at, :] = total.astype(result.dtype)
            return carry

        lax.fori_loop(0, count // tile, add, 0)
        for i, (out, at) in enumerate(task["outs"]):
            if isinstance(at, tuple):
                part = at[0].stop
                copies.out(result.at[i * part : (i + 1) * part, :], out_hbm[out].at[at])
            else:
                copies.out(result, out_hbm[out].at[at, :])
    copies.finish()


def combine(links, steps, after=(), name="combine"):
    ins, tasks, loads, stages, sends, outs = [], [], [], [], {}, []
    copies, finals, beside = 0, {}, {}
    returned = []

    def index_of(array):
        for i, other in enumerate(ins):
            if other is array:
                return i
        ins.append(array)
        return len(ins) - 1

    def send_to(where, count):
        if where not in sends:
            sends[where] = len(outs)
            outs.append([0, BF])
        at = outs[sends[where]][0]
        outs[sends[where]][0] += count
        return sends[where], slice(at, at + count)

    def places(names):
        return [
            tuple(name for k, name in enumerate(names) if mask >> k & 1)
            for mask in range(1, 1 << len(names))
        ]

    for piece, names, mode in steps:
        if mode == "raw":
            out, at = send_to(names, piece.shape[0])
            tasks.append(
                {"kind": "raw", "from": index_of(piece), "out": out, "at": at, "slot": len(loads)}
            )
            loads.append(piece)
            returned.append((out, at))
            copies += 2
            continue
        if mode == "vec":
            task = {"kind": "vec", "loads": [], "stage": len(stages)}
            width = piece.kept.shape[1]
            for array, at, count in [(piece.kept, 0, 16)] + [(b, at, 32) for b, at in piece.came]:
                task["loads"].append((index_of(array), at, count, len(loads)))
                loads.append(shape((count, width), array.dtype))
            stages += [shape((32, width), BF), shape((16, width), F32)]
            task["outs"] = [send_to(place, 32) for place in places(names)]
            task["kept"] = len(outs)
            outs.append([16, F32])
            copies += len(task["loads"]) + len(task["outs"]) + 1
            tasks.append(task)
            returned.append(task)
            continue
        split = names if mode == "split" else ()
        count, post, loops = piece.layout(split)
        width = piece.levels[0].terms[0][0].shape[1]
        if mode == "final":
            kind, key, across = (*names, 1)[:3] if isinstance(names, tuple) else (names, len(outs), 1)
            if key not in finals:
                finals[key] = len(outs)
                outs.append([0, kind])
            out = finals[key]
            at = outs[out][0]
            if across == 1:
                groups = [((), [(out, slice(at, at + count))])]
                outs[out][0] += count
            else:
                part = count // across
                places_at = [slice((at + i) * width, (at + i + 1) * width) for i in range(across)]
                groups = [((), [(out, (slice(0, part), where)) for where in places_at])]
                outs[out][0] += across
                beside[out] = part
            returned.append(out)
        elif mode == "all":
            groups = [((), [send_to(place, count) for place in places(names)])]
            kind = BF
        else:
            groups = [(place, [send_to(place, count)]) for place in places(names)]
            kind = BF
        if mode != "final":
            returned.append([out for unused, targets in groups for out in targets])
        gone = piece.gone | frozenset(split)
        for flip, targets in groups:
            task = {"kind": "sum", "flip": flip, "loads": [], "sum": [], "stage": len(stages)}
            stages.append(shape((count, width), kind))
            task["outs"] = targets
            copies += len(targets)
            for level in piece.levels:
                strides = level.owner.strides(level.gone)
                slots = []
                for t, (array, at) in enumerate(level.terms):
                    slots.append(len(loads))
                    alt, alt_at = None, at
                    if level.alt is not None:
                        buffer, alt_at = level.alt.terms[t]
                        alt = index_of(buffer)
                    task["loads"].append(
                        {
                            "in": index_of(array),
                            "alt": alt,
                            "alt_at": alt_at,
                            "alt_moving": level.alt.moving(gone) if level.alt is not None else (),
                            "choice": level.choice,
                            "at": at,
                            "moving": level.moving(gone),
                            "bases": [
                                sum(i * strides[name] for name, i in loop.items()) for loop in loops
                            ],
                            "post": post,
                            "slot": len(loads),
                        }
                    )
                    loads.append(shape((count, width), array.dtype))
                    copies += len(loops)
                task["sum"].append((level.rounded, slots))
            tasks.append(task)
    results = kernel_call(
        functools.partial(
            combine_kernel,
            links,
            tasks,
            len(ins),
            len(outs),
            len(loads),
            len(after),
        ),
        name,
        [
            shape((beside[i], count * width) if i in beside else (count, width), kind)
            for i, (count, kind) in enumerate(outs)
        ],
        loads + stages,
        copies,
    )(*ins, *after)
    came = {out: links.bring(results[out], *where) for where, out in sends.items()}
    values = []
    for (piece, names, mode), back in zip(steps, returned):
        if mode == "final":
            values.append(results[back])
        elif mode == "raw":
            values.append((came[back[0]], back[1].start))
        elif mode == "vec":
            piece.kept = results[back["kept"]]
            piece.came = [(came[out], at.start) for out, at in back["outs"]]
        else:
            if mode == "split":
                piece.gone = piece.gone | frozenset(names)
            piece.levels.append(
                Level(
                    piece, [(came[out], at.start) for out, at in back], piece.gone, mode == "all"
                )
            )
    return [results[out] for out in sends.values()], values


def touch_kernel(count, *refs):
    copies = Copies(refs[-1])
    loads = [copies.start(refs[i].at[0:16, 0:128], refs[-2].at[i]) for i in range(count)]
    for copy in loads:
        copy.wait()
    total = refs[-2][0].astype(F32)
    for i in range(1, count):
        total = total + refs[-2][i].astype(F32)
    refs[-3][...] = total


def touch(after, *pieces):
    buffers = []
    for piece in pieces:
        buffer = piece.levels[-1].terms[0][0]
        if not any(buffer is other for other in buffers):
            buffers.append(buffer)
    count = len(buffers)
    return kernel_call(
        functools.partial(touch_kernel, count),
        "touch",
        (shape((16, 128), F32),),
        (shape((count, 16, 128), BF),),
        count,
        vmem_out=1,
    )(*buffers, *after)[0]


def assemble_kernel(links, vec_ref, own_ref, x_ref, core_ref, both_ref, after_hbm, *outs):
    full_ref = outs[-2]
    piece = own_ref.shape[0] // 2
    half = own_ref.shape[1]
    x, c = links.bit(1), links.bit(0)
    for ref, dx, dc in ((own_ref, 0, 0), (x_ref, 1, 0), (core_ref, 0, 1), (both_ref, 1, 1)):
        at = ((1 - c if dc else c) * 2 + (1 - x if dx else x)) * piece
        rows = pl.ds(pl.multiple_of(at, 16), piece)
        for h in range(2):
            part = ref[h * piece : (h + 1) * piece, :]
            full_ref[rows, h * half : (h + 1) * half] = part.astype(F32)
    for i, out in enumerate(outs[:5]):
        row = jnp.concatenate([vec_ref[2 * i : 2 * i + 1, :], vec_ref[2 * i + 1 : 2 * i + 2, :]], axis=1)
        out[...] = row.reshape(out.shape)


def assemble(links, vec, near, after):
    rows, half = near[0].shape
    return kernel_call(
        functools.partial(assemble_kernel, links),
        "assemble",
        (shape((2 * half,), F32),) * 5 + (shape((2 * rows, 2 * half), F32),),
        (),
        1,
        vmem_in=5,
        vmem_out=6,
    )(vec, *near, after)


def shards(
    links,
    pixels,
    visible,
    kernels,
    class_token,
    norm1_gain,
    norm1_bias,
    norm2_gain,
    norm2_bias,
    attn_qkv,
    attn_out,
    mlp_up,
    mlp_down,
    cotangent,
):
    width = attn_out.shape[0]
    half = width // 2
    chips = cotangent.shape[0]
    group_chips, bands, patches, pix = pixels.shape
    slots = visible.shape[1]
    body = chips * slots
    depth = bands * pix
    block = width // 16
    flat = lambda a: a.reshape(-1, half)
    core_swap = lambda a: (links.swap(flat(a), 0), 0)

    pixel_rows = jnp.swapaxes(pixels, 2, 3).reshape(group_chips, depth, patches)
    kernels_own = kernels.reshape(depth, width)
    my_half, picked_far = pick_far(
        links, visible, pixel_rows, kernels_own.reshape(2, depth // 2, width)
    )
    far_half = links.swap(my_half, "band")
    picked_in = links.swap(picked_far, "band")
    picked_own, cot, gact = prepare(links, visible, pixel_rows, cotangent, mlp_down)
    far_half, cot = lax.optimization_barrier((far_half, cot))
    far_other = links.swap(far_half, 0)
    vecs = jnp.stack(
        [class_token, norm1_gain, norm1_bias, norm2_gain, norm2_bias] + [class_token] * 3
    )

    stream, n1, packed, probs, tprobs, att, mid, n2, act1, gpre1, *parts1 = forward(
        links,
        chips,
        vecs,
        picked_own,
        picked_in,
        kernels_own,
        far_half,
        far_other,
        attn_qkv,
        attn_out,
        cot,
        gact,
        mlp_up,
    )

    x, y, core, plane = (1,), ("band",), (0,), (1, "band")
    down_send, down_keep, up_send, up_keep = parts1
    down1 = Piece(
        (1, 0, "band", "h", 3, 2),
        (2,) * 6,
        block,
        [(down_keep, 0), (links.bring(down_send, 1), 0)],
        x,
    )
    up1 = Piece(
        (3, 1, 0, "band"), (2,) * 4, 4 * block, [(up_keep, 0), (links.bring(up_send, "band"), 0)], y
    )
    *sums_send, sums_keep, branch, gatt, out_rows, vec2 = mlp_back(
        links, vecs, n2, gact, act1, gpre1, mlp_up, mlp_down, mid, cot, att, attn_out, ()
    )
    both = lambda i, at: [(sums_keep, at), (links.bring(sums_send[i], 0), 0)]
    middle, end = 2 * width, 2 * width + mlp_up.shape[1] // 2
    down2 = Piece((0, 1, "band", "h", 3, 2), (2,) * 6, block, both(0, 0), core)
    up2 = Piece((0, 3, 1, "band"), (2,) * 4, 4 * block, both(1, middle), core)
    names, sizes = (0, 1, "band", 3, 2), (2,) * 5
    outp = Piece(names, sizes, block, both(2, end), core)
    block_output = jnp.concatenate(
        [
            out_rows[body : body + chips][:, None, :],
            out_rows[:body].reshape(chips, slots, width),
        ],
        axis=1,
    )
    tie, unused = combine(links, [(down1, core, "split"), (up1, core, "split")], (vec2,))
    tie, unused = combine(
        links,
        [
            (down1, y, "split"),
            (up1, x, "split"),
            (down2, x, "split"),
            (up2, y, "split"),
            (outp, (2,), "split"),
        ],
        (*tie, block_output),
    )

    gpacked, qkv_send, qkv_keep = attention_back(links, chips, gatt, packed, probs, tprobs, n1, tie)
    qkv_in = links.bring(qkv_send, 0)
    qkv = [
        Piece(names, sizes, count, [(qkv_keep, at), (qkv_in, at)], core)
        for at, count in qkv_parts(width)
    ]
    older = touch((gpacked,), down1, up1, down2, up2, outp)
    tie, unused = combine(
        links,
        [
            (down2, y, "split"),
            (up2, x, "split"),
            (qkv[0], x, "split"),
            (qkv[1], y, "split"),
            (down1, (2,), "split"),
            (up1, (3,), "split"),
            (outp, (3,), "split"),
        ],
        (older,),
    )
    kg_send, kg_keep, pgrad_own, pgrad_far, vec_keep = embed_back(
        links,
        chips,
        vecs,
        vec2,
        gpacked,
        attn_qkv,
        stream,
        branch,
        picked_own,
        picked_in,
        kernels_own,
        far_half,
        far_other,
        tie,
    )
    kg_in = links.bring(kg_send, 0)
    kg = Piece((0, "band", 1, "h"), (2,) * 4, depth // 4, [(kg_keep, 0), (kg_in, 0)], core)
    vec = Vec(vec_keep, (kg_in, 2 * depth))
    older = touch((vec_keep,), down2, up2, *qkv, down1, up1, outp)
    tie, unused = combine(
        links,
        [
            (kg, plane, "split"),
            (vec, plane, "vec"),
            (qkv[0], y, "split"),
            (qkv[1], x, "split"),
            (outp, plane, "split"),
            (down2, (2,), "split"),
            (up2, (3,), "split"),
            (down1, (3,), "split"),
        ],
        (older,),
    )
    far_grads = links.bring(flat(pgrad_far), "band")
    partly = scatter(links, 0, flat(pgrad_own), depth, visible, patches)
    up = Piece.join(up1, up2, 2)
    tie, (out_sum,) = combine(
        links,
        [
            (qkv[0], (2,), "split"),
            (qkv[1], (2,), "split"),
            (kg, (2, 3), "all"),
            (vec, (2, 3), "vec"),
            (outp, F32, "final"),
        ],
        (partly,),
    )
    scattered = scatter(links, 1, far_grads, depth, visible, patches, partly)
    pixel_grads = jnp.swapaxes(scattered.reshape(group_chips, bands, pix, patches), 2, 3)
    tie, unused = combine(
        links,
        [
            (qkv[0], (3,), "split"),
            (qkv[1], (3,), "split"),
            (up, (2,), "split"),
            (down2, (3,), "split"),
        ],
        (scattered,),
    )
    tie, (kgrad,) = combine(links, [(kg, BF, "final"), (vec, (), "vec")], tie, "finish")
    vec_sum = links.total(vec.value())
    kgrad = links.total(kgrad.astype(F32)).astype(BF)
    near = [kgrad, links.swap(kgrad, 1), links.swap(kgrad, 0), links.swap(kgrad, 0, 1)]
    tie, (*qkv_sums, up_sum, down_sum, unused) = combine(
        links,
        [
            (qkv[0], (F32, "qkv"), "final"),
            (qkv[1], (F32, "qkv"), "final"),
            (up, F32, "final"),
            (down1, (F32, "down", 2), "final"),
            (down2, (F32, "down", 2), "final"),
        ],
        (scattered,),
    )
    *vecs, kernel_grads = assemble(links, vec_sum, near, qkv_sums[0])

    weight = lambda part: jnp.swapaxes(links.last(part), 0, 1)
    return (
        block_output,
        pixel_grads,
        kernel_grads.reshape(bands, pix, width),
        vecs[2],
        vecs[0],
        vecs[1],
        vecs[3],
        vecs[4],
        weight(qkv_sums[0]),
        weight(out_sum),
        weight(up_sum),
        weight(down_sum),
    )


def solution(mesh):
    placed = (
        P("dp", "band", None, None),
        P("dp", None),
        P("band", None, None),
        P(),
        P(),
        P(),
        P(),
        P(),
        P(),
        P(),
        P(),
        P(),
        P(("dp", "band"), None, None),
    )
    return jax.shard_map(
        functools.partial(shards, Links(mesh)),
        mesh=mesh,
        in_specs=placed,
        out_specs=(
            P(("dp", "band"), None, None),
            P("dp", "band", None, None),
            P("band", None, None),
            P(),
            P(),
            P(),
            P(),
            P(),
            P("band", "dp"),
            P("band", "dp"),
            P("band", "dp"),
            P("band", "dp"),
        ),
        check_vma=False,
    )
```

profile of v0, /device:TPU:0, one launch (start us, length us, event | category | flops | bytes accessed | tf_op | source)
XLA Modules:
  0.0 218.3 jit_solution(15897305473221304155)
XLA Ops:
  0.6 5.1 %pick_far.1 = (bf16[160,768]{1,0:T(8,128)(2,1)}, bf16[320,768]{1,0:T(8,128)(2,1)}) custom-call(s32[24,64]{1,0:T(8,128)} %seen_ref.7, bf16[24,320,256]{2,1,0:T(8,128)(2,1)} %bitcast.19, bf16[2,160,768]{2,1,0:T(8,128)(2,1)} %bitcast.21), custom_call_target="tpu_custom_call" | custom-call | flops 5750000128 | bytes 1 | tf_op jit(solution)/shard_map/pick_far/pallas_call | solution.py:50
  5.7 3.0 %collective-permute-start.1 = (bf16[160,768]{1,0:T(8,128)(2,1)}, bf16[160,768]{1,0:T(8,128)(2,1)S(1)}, u32[]{:S(2)}, u32[]{:S(2)}) collective-permute-start(bf16[160,768]{1,0:T(8,128)(2,1)} %get-tuple-element.82), channel_id=1, source_target_pairs={{0,1},{1,0},{2,3},{3,2},{4,5},{5,4},{6,7},{7,6},{8,9},{9,8},{10,11... | collective-permute-start | bytes 737288 | tf_op jit(solution)/shard_map/ppermute | solution.py:1065
  8.9 12.0 %prepare.1 = (bf16[320,768]{1,0:T(8,128)(2,1)}, bf16[784,768]{1,0:T(8,128)(2,1)}, bf16[784,3072]{1,0:T(8,128)(2,1)}) custom-call(s32[24,64]{1,0:T(8,128)} %seen_ref.7, bf16[24,320,256]{2,1,0:T(8,128)(2,1)} %bitcast.20, bf16[12,65,768]{2,1,0:T(8,128)(2,1)} %cot_hbm.1, bf16[3072,768]{1,0:T(8,128)(2,1)} %down_hbm.3), custom_call_target="tpu_custom_call" | custom-call | flops 12650000384 | bytes 1 | tf_op jit(solution)/shard_map/prepare/pallas_call | solution.py:50
  21.7 3.7 %collective-permute-done.xr_hbm = bf16[320,768]{1,0:T(8,128)(2,1)S(1)} collective-permute-done((bf16[320,768]{1,0:T(8,128)(2,1)}, bf16[320,768]{1,0:T(8,128)(2,1)S(1)}, u32[]{:S(2)}, u32[]{:S(2)}) %collective-permute-start) | collective-permute-done | bytes 491552 | tf_op jit(solution)/shard_map/ppermute | solution.py:1065
  25.5 0.8 copy-done.17
  26.3 31.7 %encoder_forward.1 = (f32[784,768]{1,0:T(8,128)}, bf16[784,768]{1,0:T(8,128)(2,1)}, bf16[784,2304]{1,0:T(8,128)(2,1)}, bf16[12,6,80,128]{3,2,1,0:T(8,128)(2,1)},...) custom-call(f32[8,768]{1,0:T(8,128)} %stack.26.vecs_ref, ...), custom_call_target="tpu_custom_call" | custom-call | flops 35649998848 | bytes 1 | tf_op jit(solution)/shard_map/encoder_forward/pallas_call | solution.py:50
  58.1 1.7 collective-permute-start.3
  59.8 1.6 collective-permute-start.4
  61.4 28.5 %mlp_back.1 = (bf16[1536,384]{1,0:T(8,128)(2,1)}, bf16[1536,384]{1,0:T(8,128)(2,1)}, bf16[768,384]{1,0:T(8,128)(2,1)}, bf16[3840,384]{1,0:T(8,128)(2,1)}, bf16[7...) custom-call(f32[8,768]{1,0:T(8,128)} %stack.26.vecs_ref, ...), custom_call_target="tpu_custom_call" | custom-call | flops 36800000000 | bytes 1 | tf_op jit(solution)/shard_map/mlp_back/pallas_call | solution.py:50
  90.4 1.0 copy-done.14
  91.4 2.8 %combine.7.refs_9_ = bf16[1536,384]{1,0:T(8,128)(2,1)} custom-call(bf16[1536,384]{1,0:T(8,128)(2,1)} %get-tuple-element.99.refs_0_.refs_7_.refs_15_.refs_18_, bf16[1536,384]{1,0:T(8,128)(2,1)} %copy-done.14, bf16[1536,384]{1,0:T(8,128)(2,1)} %get-tuple-element.101.refs_2_.refs_3_.refs_10_.refs_8_.refs_9_, ...), custom_call_target="tpu_custom_call" | custom-call | flops 13799999488 | bytes 1 | tf_op jit(solution)/shard_map/combine/pallas_call | solution.py:50
  94.9 1.4 pad_maximum_fusion.refs_10_
  96.3 1.8 collective-permute-done.8.refs_8_.refs_12_.refs_11_
  99.0 3.6 %combine.8 = (bf16[1152,384]{1,0:T(8,128)(2,1)}, bf16[1152,384]{1,0:T(8,128)(2,1)}, bf16[384,384]{1,0:T(8,128)(2,1)}) custom-call(bf16[1536,384]{1,0:T(8,128)(2,1)} %get-tuple-element.99.refs_0_.refs_7_.refs_15_.refs_18_, bf16[1536,384]{1,0:T(8,128)(2,1)} %copy-done.14, bf16[1536,384]{1,0:T(8,128)(2,1)} %collective-permute-done.5.refs_2_.refs_9_.refs_17_.refs_12_.refs_13_, ...), custom_call_target="tpu_custom_call" | custom-call | flops 13799999488 | bytes 1 | tf_op jit(solution)/shard_map/combine/pallas_call | solution.py:50
  102.5 1.6 collective-permute-start.12
  105.2 17.9 %attention_back.1 = (bf16[784,2304]{1,0:T(8,128)(2,1)}, bf16[2304,384]{1,0:T(8,128)(2,1)}, bf16[2304,384]{1,0:T(8,128)(2,1)}) custom-call(bf16[784,768]{1,0:T(8,128)(2,1)} %get-tuple-element.94.gatt_hbm, bf16[784,2304]{1,0:T(8,128)(2,1)} %get-tuple-element.95.packed_hbm, bf16[12,6,80,128]{3,2,1,0:T(8,128)(2,1)} %get-tuple-element.96.probs_hbm, ...), custom_call_target="tpu_custom_call" | custom-call | flops 20700000256 | bytes 1 | tf_op jit(solution)/shard_map/attention_back/pallas_call | solution.py:50
  123.2 2.7 %collective-permute-done.10.refs_0_.refs_4_.refs_14_.refs_11_.refs_12_ = bf16[1152,384]{1,0:T(8,128)(2,1)} collective-permute-done((bf16[1152,384]{1,0:T(8,128)(2,1)}, bf16[1152,384]{1,0:T(8,128)(2,1)}, u32[]{:S(2)}, u32[]{:S(2)}) %collective-permute-start.10) | collective-permute-done | bytes 884768 | tf_op jit(solution)/shard_map/ppermute | solution.py:1065
  126.1 1.3 touch.2.refs_14_
  127.5 1.2 copy-done.13
  128.7 3.7 %combine.9 = (bf16[896,384]{1,0:T(8,128)(2,1)}, bf16[1024,384]{1,0:T(8,128)(2,1)}, bf16[192,384]{1,0:T(8,128)(2,1)}, bf16[384,384]{1,0:T(8,128)(2,1)}) custom-call(bf16[3840,384]{1,0:T(8,128)(2,1)} %get-tuple-element.103.refs_5_.refs_0_.refs_7_.refs_10_.refs_8_, bf16[1536,384]{1,0:T(8,128)(2,1)} %collective-permute-done.6.refs_6_.refs_1_.refs_11_.refs_16_.refs_21_, ...), custom_call_target="tpu_custom_call" | custom-call | flops 13799999488 | bytes 1 | tf_op jit(solution)/shard_map/combine/pallas_call | solution.py:50
  132.9 2.6 %collective-permute-start.17 = (bf16[384,384]{1,0:T(8,128)(2,1)}, bf16[384,384]{1,0:T(8,128)(2,1)S(1)}, u32[]{:S(2)}, u32[]{:S(2)}) collective-permute-start(bf16[384,384]{1,0:T(8,128)(2,1)} %get-tuple-element.118.rest_3_), channel_id=1, source_target_pairs={{0,16},{2,18},{4,20},{6,22},{8,24},{10,26},{12,28},{14,30},{16,0},... | collective-permute-start | bytes 884744 | tf_op jit(solution)/shard_map/ppermute | solution.py:1063
  135.5 1.6 collective-permute-start.16
  137.0 1.1 collective-permute-start.15
  138.2 13.3 %embed_back.1 = (bf16[672,384]{1,0:T(8,128)(2,1)}, bf16[640,384]{1,0:T(8,128)(2,1)}, bf16[2,320,384]{2,1,0:T(8,128)(2,1)}, bf16[2,320,384]{2,1,0:T(8,128)(2,1)}, f32[16,384]{1,0:T(8,128)}) custom-call(f32[8,768]{1,0:T(8,128)} %stack.26.vecs_ref, f32[2,768]{1,0:T(2,128)} %get-tuple-element.93.refs_4_.vec2_ref, ...), custom_call_target="tpu_custom_call" | custom-call | flops 16099999744 | bytes 1 | tf_op jit(solution)/shard_map/embed_back/pallas_call | solution.py:50
  152.4 3.2 %collective-permute-done.15.refs_1_.refs_5_.refs_2_ = bf16[1024,384]{1,0:T(8,128)(2,1)S(1)} collective-permute-done((bf16[1024,384]{1,0:T(8,128)(2,1)}, bf16[1024,384]{1,0:T(8,128)(2,1)S(1)}, u32[]{:S(2)}, u32[]{:S(2)}) %collective-permute-start.15) | collective-permute-done | bytes 786464 | tf_op jit(solution)/shard_map/ppermute | solution.py:1063
  155.6 0.9 copy-done.15
  156.5 1.3 touch.3.refs_19_
  157.9 0.8 copy-done.1
  158.7 3.7 %combine.10 = (bf16[496,384]{1,0:T(8,128)(2,1)}, bf16[560,384]{1,0:T(8,128)(2,1)}, bf16[240,384]{1,0:T(8,128)(2,1)}, f32[16,384]{1,0:T(8,128)}, bf16[192,384]{1,0:T(8,128)(2,1)}, /*index=5*/bf16[288,384]{1,0:T(8,128)(2,1)}) custom-call(bf16[640,384]{1,0:T(8,128)(2,1)} %get-tuple-element.121.refs_0_.refs_6_, bf16[672,384]{1,0:T(8,128)(2,1)} %copy-done.1, ...), custom_call_target="tpu_custom_call" | custom-call | flops 13799999488 | bytes 1 | tf_op jit(solution)/shard_map/combine/pallas_call | solution.py:50
  162.4 1.5 collective-permute-start.21
  164.5 1.5 collective-permute-start.20
  166.0 4.5 %scatter.2.rest_0_.refs_14_ = f32[24,320,256]{2,1,0:T(8,128)} custom-call(s32[24,64]{1,0:T(8,128)} %seen_ref.7, bf16[640,384]{1,0:T(8,128)(2,1)} %bitcast.27), custom_call_target="tpu_custom_call" | custom-call | flops 4600000000 | bytes 1 | tf_op jit(solution)/shard_map/scatter/pallas_call | solution.py:50
  170.6 1.7 collective-permute-start.26
  172.6 3.0 %collective-permute-done.19.refs_5_.refs_6_.refs_2_.refs_7_ = bf16[496,384]{1,0:T(8,128)(2,1)S(1)} collective-permute-done((bf16[496,384]{1,0:T(8,128)(2,1)}, bf16[496,384]{1,0:T(8,128)(2,1)S(1)}, u32[]{:S(2)}, u32[]{:S(2)}) %collective-permute-start.19) | collective-permute-done | bytes 380960 | tf_op jit(solution)/shard_map/ppermute | solution.py:1063
  175.6 1.8 collective-permute-done.20.refs_3_
  177.4 0.8 copy-done.2
  178.1 2.7 %combine.11 = (bf16[480,384]{1,0:T(8,128)(2,1)}, bf16[192,384]{1,0:T(8,128)(2,1)}, bf16[192,384]{1,0:T(8,128)(2,1)}, f32[16,384]{1,0:T(8,128)}, f32[48,384]{1,0:T(8,128)}) custom-call(bf16[2304,384]{1,0:T(8,128)(2,1)} %get-tuple-element.113.refs_5_.refs_3_.refs_0_, bf16[2304,384]{1,0:T(8,128)(2,1)} %copy-done.13, bf16[1024,384]{1,0:T(8,128)(2,1)} %copy-done.15, ...), custom_call_target="tpu_custom_call" | custom-call | flops 13799999488 | bytes 1 | tf_op jit(solution)/shard_map/combine/pallas_call | solution.py:50
  181.3 3.6 %collective-permute-start.24 = (bf16[192,384]{1,0:T(8,128)(2,1)}, bf16[192,384]{1,0:T(8,128)(2,1)S(1)}, u32[]{:S(2)}, u32[]{:S(2)}) collective-permute-start(bf16[192,384]{1,0:T(8,128)(2,1)} %get-tuple-element.130), channel_id=1, source_target_pairs={{0,24},{2,26},{4,28},{6,30},{8,16},{10,18},{12,20},{14,22},{16,8},... | collective-permute-start | bytes 442376 | tf_op jit(solution)/shard_map/ppermute | solution.py:1063
  184.9 4.5 %scatter.3.refs_18_.refs_23_ = f32[24,320,256]{2,1,0:T(8,128)} custom-call(s32[24,64]{1,0:T(8,128)} %seen_ref.7, bf16[640,384]{1,0:T(8,128)(2,1)} %collective-permute-done.13.grad_hbm, f32[24,320,256]{2,1,0:T(8,128)} %scatter.2.rest_0_.refs_14_), custom_call_target="tpu_custom_call", output_to_operand_aliasing={{}: (2, {})} | custom-call | flops 4600000000 | bytes 1 | tf_op jit(solution)/shard_map/scatter/pallas_call | solution.py:50
  189.4 9.2 %collective-permute-done.22.refs_4_.refs_5_ = bf16[480,384]{1,0:T(8,128)(2,1)S(1)} collective-permute-done((bf16[480,384]{1,0:T(8,128)(2,1)}, bf16[480,384]{1,0:T(8,128)(2,1)S(1)}, u32[]{:S(2)}, u32[]{:S(2)}) %collective-permute-start.22) | collective-permute-done | bytes 368672 | tf_op jit(solution)/shard_map/ppermute | solution.py:1063
  198.7 0.8 copy-done.4
  199.4 2.4 %combine.12 = (bf16[240,384]{1,0:T(8,128)(2,1)}, bf16[192,384]{1,0:T(8,128)(2,1)}) custom-call(bf16[2304,384]{1,0:T(8,128)(2,1)} %get-tuple-element.113.refs_5_.refs_3_.refs_0_, bf16[2304,384]{1,0:T(8,128)(2,1)} %copy-done.13, bf16[1024,384]{1,0:T(8,128)(2,1)} %copy-done.15, bf16[560,384]{1,0:T(8,128)(2,1)} %copy-done.2, bf16[480,384]{1,0:T(8,128)(2,1)} %copy-done.4, ...), custom_call_target="tpu_custom_call" | custom-call | flops 13799999488 | bytes 1 | tf_op jit(solution)/shard_map/combine/pallas_call | solution.py:50
  202.3 1.6 collective-permute-start.31
  204.6 2.2 %finish.1 = (bf16[160,384]{1,0:T(8,128)(2,1)}, f32[16,384]{1,0:T(8,128)}) custom-call(bf16[640,384]{1,0:T(8,128)(2,1)} %get-tuple-element.121.refs_0_.refs_6_, bf16[672,384]{1,0:T(8,128)(2,1)} %copy-done.1, bf16[496,384]{1,0:T(8,128)(2,1)} %copy-done.3, bf16[560,384]{1,0:T(8,128)(2,1)} %copy-done.2, bf16[240,384]{1,0:T(8,128)(2,1)} %copy-done.5, ...), custom_call_target="tpu_custom_call" | custom-call | flops 575000000 | bytes 1 | tf_op jit(solution)/shard_map/finish/pallas_call | solution.py:50
  206.9 2.3 %collective-permute-start.28 = (bf16[160,384]{1,0:T(8,128)(2,1)}, bf16[160,384]{1,0:T(8,128)(2,1)S(1)}, u32[]{:S(2)}, u32[]{:S(2)}) collective-permute-start(bf16[160,384]{1,0:T(8,128)(2,1)} %get-tuple-element.137.own_ref), channel_id=1, source_target_pairs={{0,2},{2,0},{4,6},{6,4},{8,10},{10,8},{12,14},{14,12},{16,18},{18,... | collective-permute-start | bytes 368648 | tf_op jit(solution)/shard_map/ppermute | solution.py:1063
  209.2 2.2 %collective-permute-done.30.refs_5_ = bf16[240,384]{1,0:T(8,128)(2,1)S(1)} collective-permute-done((bf16[240,384]{1,0:T(8,128)(2,1)}, bf16[240,384]{1,0:T(8,128)(2,1)S(1)}, u32[]{:S(2)}, u32[]{:S(2)}) %collective-permute-start.30) | collective-permute-done | bytes 184352 | tf_op jit(solution)/shard_map/ppermute | solution.py:1063
  212.2 2.8 %combine.13 = (f32[144,384]{1,0:T(8,128)}, f32[192,384]{1,0:T(8,128)}, f32[48,1536]{1,0:T(8,128)}) custom-call(bf16[2304,384]{1,0:T(8,128)(2,1)} %get-tuple-element.113.refs_5_.refs_3_.refs_0_, bf16[2304,384]{1,0:T(8,128)(2,1)} %copy-done.13, bf16[1024,384]{1,0:T(8,128)(2,1)} %copy-done.15, bf16[560,384]{1,0:T(8,128)(2,1)} %copy-done.2, ...), custom_call_target="tpu_custom_call" | custom-call | flops 13799999488 | bytes 1 | tf_op jit(solution)/shard_map/combine/pallas_call | solution.py:50
  216.0 2.1 assemble.1
  (107 shorter events, 10.1 us)
Async XLA Ops:
  5.7 15.2 %collective-permute-start.1 = (bf16[160,768]{1,0:T(8,128)(2,1)}, bf16[160,768]{1,0:T(8,128)(2,1)S(1)}, u32[]{:S(2)}, u32[]{:S(2)}) collective-permute-start(bf16[160,768]{1,0:T(8,128)(2,1)} %get-tuple-element.82), channel_id=1, source_target_pairs={{0,1},{1,0},{2,3},{3,2},{4,5},{5,4},{6,7},{7,6},{8,9},{9,8},{10,11... | collective-permute-start | bytes 737288 | tf_op jit(solution)/shard_map/ppermute | solution.py:1065
  8.7 12.2 %copy-start.8 = (f32[768]{0:T(1024)S(1)}, f32[768]{0:T(1024)}, u32[]{:S(2)}) copy-start(f32[768]{0:T(1024)} %param.16) | copy-start | bytes 9220
  8.7 12.3 %copy-start.9 = (f32[768]{0:T(1024)S(1)}, f32[768]{0:T(1024)}, u32[]{:S(2)}) copy-start(f32[768]{0:T(1024)} %param.17) | copy-start | bytes 9220
  8.7 12.3 %copy-start.10 = (f32[768]{0:T(1024)S(1)}, f32[768]{0:T(1024)}, u32[]{:S(2)}) copy-start(f32[768]{0:T(1024)} %param.18) | copy-start | bytes 9220
  8.7 12.3 %copy-start.11 = (f32[768]{0:T(1024)S(1)}, f32[768]{0:T(1024)}, u32[]{:S(2)}) copy-start(f32[768]{0:T(1024)} %param.19) | copy-start | bytes 9220
  8.7 12.3 %copy-start.12 = (f32[768]{0:T(1024)S(1)}, f32[768]{0:T(1024)}, u32[]{:S(2)}) copy-start(f32[768]{0:T(1024)} %param.20) | copy-start | bytes 9220
  8.8 16.7 %collective-permute-start = (bf16[320,768]{1,0:T(8,128)(2,1)}, bf16[320,768]{1,0:T(8,128)(2,1)S(1)}, u32[]{:S(2)}, u32[]{:S(2)}) collective-permute-start(bf16[320,768]{1,0:T(8,128)(2,1)} %get-tuple-element.81), channel_id=1, source_target_pairs={{0,1},{1,0},{2,3},{3,2},{4,5},{5,4},{6,7},{7,6},{8,9},{9,8},{10,11... | collective-permute-start | bytes 1474568 | tf_op jit(solution)/shard_map/ppermute | solution.py:1065
  20.9 4.6 %copy-start.19 = (bf16[160,768]{1,0:T(8,128)(2,1)}, bf16[160,768]{1,0:T(8,128)(2,1)S(1)}, u32[]{:S(2)}) copy-start(bf16[160,768]{1,0:T(8,128)(2,1)S(1)} %collective-permute-done.1.half_hbm) | copy-start | bytes 737284
  20.9 4.6 %collective-permute-start.2 = (bf16[160,768]{1,0:T(8,128)(2,1)S(1)}, bf16[160,768]{1,0:T(8,128)(2,1)S(1)}, u32[]{:S(2)}, u32[]{:S(2)}) collective-permute-start(bf16[160,768]{1,0:T(8,128)(2,1)S(1)} %collective-permute-done.1.half_hbm), channel_id=1, source_target_pairs={{0,2},{2,0},{4,6},{6,4},{8,10},{10,8},{12,14},{14,12},{16,18},{18,... | collective-permute-start | bytes 737288 | tf_op jit(solution)/shard_map/ppermute | solution.py:1063
  58.1 32.3 %collective-permute-start.3 = (bf16[1536,384]{1,0:T(8,128)(2,1)}, bf16[1536,384]{1,0:T(8,128)(2,1)S(1)}, u32[]{:S(2)}, u32[]{:S(2)}) collective-permute-start(bf16[1536,384]{1,0:T(8,128)(2,1)} %get-tuple-element.100), channel_id=1, source_target_pairs={{0,4},{2,6},{4,0},{6,2},{8,12},{10,14},{12,8},{14,10},{16,20},{18,... | collective-permute-start | bytes 3538952 | tf_op jit(solution)/shard_map/ppermute | solution.py:1063
  59.8 30.6 %collective-permute-start.4 = (bf16[1536,384]{1,0:T(8,128)(2,1)}, bf16[1536,384]{1,0:T(8,128)(2,1)}, u32[]{:S(2)}, u32[]{:S(2)}) collective-permute-start(bf16[1536,384]{1,0:T(8,128)(2,1)} %get-tuple-element.102), channel_id=1, source_target_pairs={{0,1},{1,0},{2,3},{3,2},{4,5},{5,4},{6,7},{7,6},{8,9},{9,8},{10,11... | collective-permute-start | bytes 3538952 | tf_op jit(solution)/shard_map/ppermute | solution.py:1065
  89.8 8.3 %collective-permute-start.6 = (bf16[1536,384]{1,0:T(8,128)(2,1)}, bf16[1536,384]{1,0:T(8,128)(2,1)}, u32[]{:S(2)}, u32[]{:S(2)}) collective-permute-start(bf16[1536,384]{1,0:T(8,128)(2,1)} %get-tuple-element.104), channel_id=1, source_target_pairs={{0,2},{2,0},{4,6},{6,4},{8,10},{10,8},{12,14},{14,12},{16,18},{18,... | collective-permute-start | bytes 3538952 | tf_op jit(solution)/shard_map/ppermute | solution.py:1063
  89.9 8.2 %collective-permute-start.7 = (bf16[1536,384]{1,0:T(8,128)(2,1)}, bf16[1536,384]{1,0:T(8,128)(2,1)}, u32[]{:S(2)}, u32[]{:S(2)}) collective-permute-start(bf16[1536,384]{1,0:T(8,128)(2,1)} %get-tuple-element.105), channel_id=1, source_target_pairs={{0,2},{2,0},{4,6},{6,4},{8,10},{10,8},{12,14},{14,12},{16,18},{18,... | collective-permute-start | bytes 3538952 | tf_op jit(solution)/shard_map/ppermute | solution.py:1063
  91.4 3.4 %copy-start = (bf16[784,768]{1,0:T(8,128)(2,1)S(1)}, bf16[784,768]{1,0:T(8,128)(2,1)}, u32[]{:S(2)}) copy-start(bf16[784,768]{1,0:T(8,128)(2,1)} %get-tuple-element.92) | copy-start | bytes 3612676
  94.2 4.1 %collective-permute-start.5 = (bf16[1536,384]{1,0:T(8,128)(2,1)}, bf16[1536,384]{1,0:T(8,128)(2,1)}, u32[]{:S(2)}, u32[]{:S(2)}) collective-permute-start(bf16[1536,384]{1,0:T(8,128)(2,1)} %combine.7.refs_9_), channel_id=1, source_target_pairs={{0,2},{2,0},{4,6},{6,4},{8,10},{10,8},{12,14},{14,12},{16,18},{18,... | collective-permute-start | bytes 3538952 | tf_op jit(solution)/shard_map/ppermute | solution.py:1063
  94.4 3.8 %collective-permute-start.8 = (bf16[768,384]{1,0:T(8,128)(2,1)}, bf16[768,384]{1,0:T(8,128)(2,1)S(1)}, u32[]{:S(2)}, u32[]{:S(2)}) collective-permute-start(bf16[768,384]{1,0:T(8,128)(2,1)} %get-tuple-element.106), channel_id=1, source_target_pairs={{0,2},{2,0},{4,6},{6,4},{8,10},{10,8},{12,14},{14,12},{16,18},{18,... | collective-permute-start | bytes 1769480 | tf_op jit(solution)/shard_map/ppermute | solution.py:1063
  102.5 20.6 %collective-permute-start.12 = (bf16[384,384]{1,0:T(8,128)(2,1)}, bf16[384,384]{1,0:T(8,128)(2,1)}, u32[]{:S(2)}, u32[]{:S(2)}) collective-permute-start(bf16[384,384]{1,0:T(8,128)(2,1)} %get-tuple-element.109.rest_2_), channel_id=1, source_target_pairs={{0,8},{2,10},{4,12},{6,14},{8,0},{10,2},{12,4},{14,6},{16,24},{18,... | collective-permute-start | bytes 884744 | tf_op jit(solution)/shard_map/ppermute | solution.py:1063
  104.1 21.7 %collective-permute-start.10 = (bf16[1152,384]{1,0:T(8,128)(2,1)}, bf16[1152,384]{1,0:T(8,128)(2,1)}, u32[]{:S(2)}, u32[]{:S(2)}) collective-permute-start(bf16[1152,384]{1,0:T(8,128)(2,1)} %get-tuple-element.107.rest_0_), channel_id=1, source_target_pairs={{0,1},{1,0},{2,3},{3,2},{4,5},{5,4},{6,7},{7,6},{8,9},{9,8},{10,11... | collective-permute-start | bytes 2654216 | tf_op jit(solution)/shard_map/ppermute | solution.py:1065
  104.7 21.4 %collective-permute-start.9 = (bf16[1152,384]{1,0:T(8,128)(2,1)}, bf16[1152,384]{1,0:T(8,128)(2,1)}, u32[]{:S(2)}, u32[]{:S(2)}) collective-permute-start(bf16[1152,384]{1,0:T(8,128)(2,1)} %get-tuple-element.108.rest_1_), channel_id=1, source_target_pairs={{0,4},{2,6},{4,0},{6,2},{8,12},{10,14},{12,8},{14,10},{16,20},{18,... | collective-permute-start | bytes 2654216 | tf_op jit(solution)/shard_map/ppermute | solution.py:1063
  123.1 4.4 %collective-permute-start.11 = (bf16[2304,384]{1,0:T(8,128)(2,1)}, bf16[2304,384]{1,0:T(8,128)(2,1)S(1)}, u32[]{:S(2)}, u32[]{:S(2)}) collective-permute-start(bf16[2304,384]{1,0:T(8,128)(2,1)} %get-tuple-element.114), channel_id=1, source_target_pairs={{0,2},{2,0},{4,6},{6,4},{8,10},{10,8},{12,14},{14,12},{16,18},{18,... | collective-permute-start | bytes 5308424 | tf_op jit(solution)/shard_map/ppermute | solution.py:1063
  132.4 19.6 %collective-permute-start.18 = (bf16[192,384]{1,0:T(8,128)(2,1)}, bf16[192,384]{1,0:T(8,128)(2,1)S(1)}, u32[]{:S(2)}, u32[]{:S(2)}) collective-permute-start(bf16[192,384]{1,0:T(8,128)(2,1)} %get-tuple-element.117.rest_2_), channel_id=1, source_target_pairs={{0,8},{2,10},{4,12},{6,14},{8,0},{10,2},{12,4},{14,6},{16,24},{18,... | collective-permute-start | bytes 442376 | tf_op jit(solution)/shard_map/ppermute | solution.py:1063
  132.9 19.1 %collective-permute-start.17 = (bf16[384,384]{1,0:T(8,128)(2,1)}, bf16[384,384]{1,0:T(8,128)(2,1)S(1)}, u32[]{:S(2)}, u32[]{:S(2)}) collective-permute-start(bf16[384,384]{1,0:T(8,128)(2,1)} %get-tuple-element.118.rest_3_), channel_id=1, source_target_pairs={{0,16},{2,18},{4,20},{6,22},{8,24},{10,26},{12,28},{14,30},{16,0},... | collective-permute-start | bytes 884744 | tf_op jit(solution)/shard_map/ppermute | solution.py:1063
  135.5 16.9 %collective-permute-start.16 = (bf16[896,384]{1,0:T(8,128)(2,1)}, bf16[896,384]{1,0:T(8,128)(2,1)}, u32[]{:S(2)}, u32[]{:S(2)}) collective-permute-start(bf16[896,384]{1,0:T(8,128)(2,1)} %get-tuple-element.115.rest_0_), channel_id=1, source_target_pairs={{0,1},{1,0},{2,3},{3,2},{4,5},{5,4},{6,7},{7,6},{8,9},{9,8},{10,11... | collective-permute-start | bytes 2064392 | tf_op jit(solution)/shard_map/ppermute | solution.py:1065
  137.0 18.6 %collective-permute-start.15 = (bf16[1024,384]{1,0:T(8,128)(2,1)}, bf16[1024,384]{1,0:T(8,128)(2,1)S(1)}, u32[]{:S(2)}, u32[]{:S(2)}) collective-permute-start(bf16[1024,384]{1,0:T(8,128)(2,1)} %get-tuple-element.116.rest_1_), channel_id=1, source_target_pairs={{0,4},{2,6},{4,0},{6,2},{8,12},{10,14},{12,8},{14,10},{16,20},{18,... | collective-permute-start | bytes 2359304 | tf_op jit(solution)/shard_map/ppermute | solution.py:1063
  151.5 33.4 %collective-permute-start.13 = (bf16[640,384]{1,0:T(8,128)(2,1)}, bf16[640,384]{1,0:T(8,128)(2,1)}, u32[]{:S(2)}, u32[]{:S(2)}) collective-permute-start(bf16[640,384]{1,0:T(8,128)(2,1)} %bitcast.24), channel_id=1, source_target_pairs={{0,1},{1,0},{2,3},{3,2},{4,5},{5,4},{6,7},{7,6},{8,9},{9,8},{10,11... | collective-permute-start | bytes 1474568 | tf_op jit(solution)/shard_map/ppermute | solution.py:1065
  152.0 3.6 %copy-start.24 = (bf16[192,384]{1,0:T(8,128)(2,1)}, bf16[192,384]{1,0:T(8,128)(2,1)S(1)}, u32[]{:S(2)}) copy-start(bf16[192,384]{1,0:T(8,128)(2,1)S(1)} %collective-permute-done.18.refs_2_.refs_18_.refs_20_) | copy-start | bytes 442372
  152.0 5.8 %collective-permute-start.14 = (bf16[672,384]{1,0:T(8,128)(2,1)}, bf16[672,384]{1,0:T(8,128)(2,1)S(1)}, u32[]{:S(2)}, u32[]{:S(2)}) collective-permute-start(bf16[672,384]{1,0:T(8,128)(2,1)} %get-tuple-element.122), channel_id=1, source_target_pairs={{0,2},{2,0},{4,6},{6,4},{8,10},{10,8},{12,14},{14,12},{16,18},{18,... | collective-permute-start | bytes 1548296 | tf_op jit(solution)/shard_map/ppermute | solution.py:1063
  152.1 3.6 %copy-start.18 = (bf16[384,384]{1,0:T(8,128)(2,1)}, bf16[384,384]{1,0:T(8,128)(2,1)S(1)}, u32[]{:S(2)}) copy-start(bf16[384,384]{1,0:T(8,128)(2,1)S(1)} %collective-permute-done.17.refs_3_.refs_10_.refs_13_.refs_15_.refs_16_) | copy-start | bytes 884740
  162.4 9.8 %collective-permute-start.21 = (bf16[240,384]{1,0:T(8,128)(2,1)}, bf16[240,384]{1,0:T(8,128)(2,1)S(1)}, u32[]{:S(2)}, u32[]{:S(2)}) collective-permute-start(bf16[240,384]{1,0:T(8,128)(2,1)} %get-tuple-element.126), channel_id=1, source_target_pairs={{0,5},{1,4},{2,7},{3,6},{4,1},{5,0},{6,3},{7,2},{8,13},{9,12},{10,... | collective-permute-start | bytes 552968 | tf_op jit(solution)/shard_map/ppermute | solution.py:1069
  163.9 11.6 %collective-permute-start.19 = (bf16[496,384]{1,0:T(8,128)(2,1)}, bf16[496,384]{1,0:T(8,128)(2,1)S(1)}, u32[]{:S(2)}, u32[]{:S(2)}) collective-permute-start(bf16[496,384]{1,0:T(8,128)(2,1)} %get-tuple-element.124), channel_id=1, source_target_pairs={{0,4},{2,6},{4,0},{6,2},{8,12},{10,14},{12,8},{14,10},{16,20},{18,... | collective-permute-start | bytes 1142792 | tf_op jit(solution)/shard_map/ppermute | solution.py:1063
  164.5 12.9 %collective-permute-start.20 = (bf16[560,384]{1,0:T(8,128)(2,1)}, bf16[560,384]{1,0:T(8,128)(2,1)S(1)}, u32[]{:S(2)}, u32[]{:S(2)}) collective-permute-start(bf16[560,384]{1,0:T(8,128)(2,1)} %get-tuple-element.125), channel_id=1, source_target_pairs={{0,1},{1,0},{2,3},{3,2},{4,5},{5,4},{6,7},{7,6},{8,9},{9,8},{10,11... | collective-permute-start | bytes 1290248 | tf_op jit(solution)/shard_map/ppermute | solution.py:1065
  166.0 4.6 %copy-start.26 = (bf16[192,384]{1,0:T(8,128)(2,1)S(1)}, bf16[192,384]{1,0:T(8,128)(2,1)}, u32[]{:S(2)}) copy-start(bf16[192,384]{1,0:T(8,128)(2,1)} %get-tuple-element.133) | copy-start | bytes 442372
  166.0 6.2 %copy-start.22 = (bf16[288,384]{1,0:T(8,128)(2,1)S(1)}, bf16[288,384]{1,0:T(8,128)(2,1)}, u32[]{:S(2)}) copy-start(bf16[288,384]{1,0:T(8,128)(2,1)} %get-tuple-element.132) | copy-start | bytes 663556
  170.6 18.8 %collective-permute-start.26 = (bf16[192,384]{1,0:T(8,128)(2,1)S(1)}, bf16[192,384]{1,0:T(8,128)(2,1)S(1)}, u32[]{:S(2)}, u32[]{:S(2)}) collective-permute-start(bf16[192,384]{1,0:T(8,128)(2,1)S(1)} %copy-done.26), channel_id=1, source_target_pairs={{0,8},{2,10},{4,12},{6,14},{8,0},{10,2},{12,4},{14,6},{16,24},{18,... | collective-permute-start | bytes 442376 | tf_op jit(solution)/shard_map/ppermute | solution.py:1063
  172.2 5.1 %copy-start.5 = (bf16[240,384]{1,0:T(8,128)(2,1)}, bf16[240,384]{1,0:T(8,128)(2,1)S(1)}, u32[]{:S(2)}) copy-start(bf16[240,384]{1,0:T(8,128)(2,1)S(1)} %collective-permute-done.21.refs_8_.refs_4_) | copy-start | bytes 552964
  172.2 17.2 %collective-permute-start.25 = (bf16[288,384]{1,0:T(8,128)(2,1)S(1)}, bf16[288,384]{1,0:T(8,128)(2,1)S(1)}, u32[]{:S(2)}, u32[]{:S(2)}) collective-permute-start(bf16[288,384]{1,0:T(8,128)(2,1)S(1)} %copy-done.22), channel_id=1, source_target_pairs={{0,16},{2,18},{4,20},{6,22},{8,24},{10,26},{12,28},{14,30},{16,0},... | collective-permute-start | bytes 663560 | tf_op jit(solution)/shard_map/ppermute | solution.py:1063
  175.6 1.8 copy-start.3
  180.8 23.1 %collective-permute-start.23 = (bf16[192,384]{1,0:T(8,128)(2,1)}, bf16[192,384]{1,0:T(8,128)(2,1)S(1)}, u32[]{:S(2)}, u32[]{:S(2)}) collective-permute-start(bf16[192,384]{1,0:T(8,128)(2,1)} %get-tuple-element.129), channel_id=1, source_target_pairs={{0,16},{2,18},{4,20},{6,22},{8,24},{10,26},{12,28},{14,30},{16,0},... | collective-permute-start | bytes 442376 | tf_op jit(solution)/shard_map/ppermute | solution.py:1063
  181.3 22.6 %collective-permute-start.24 = (bf16[192,384]{1,0:T(8,128)(2,1)}, bf16[192,384]{1,0:T(8,128)(2,1)S(1)}, u32[]{:S(2)}, u32[]{:S(2)}) collective-permute-start(bf16[192,384]{1,0:T(8,128)(2,1)} %get-tuple-element.130), channel_id=1, source_target_pairs={{0,24},{2,26},{4,28},{6,30},{8,16},{10,18},{12,20},{14,22},{16,8},... | collective-permute-start | bytes 442376 | tf_op jit(solution)/shard_map/ppermute | solution.py:1063
  184.9 13.8 %collective-permute-start.22 = (bf16[480,384]{1,0:T(8,128)(2,1)}, bf16[480,384]{1,0:T(8,128)(2,1)S(1)}, u32[]{:S(2)}, u32[]{:S(2)}) collective-permute-start(bf16[480,384]{1,0:T(8,128)(2,1)} %get-tuple-element.128), channel_id=1, source_target_pairs={{0,8},{2,10},{4,12},{6,14},{8,0},{10,2},{12,4},{14,6},{16,24},{18,... | collective-permute-start | bytes 1105928 | tf_op jit(solution)/shard_map/ppermute | solution.py:1063
  189.4 9.2 %copy-start.25 = (bf16[192,384]{1,0:T(8,128)(2,1)}, bf16[192,384]{1,0:T(8,128)(2,1)S(1)}, u32[]{:S(2)}) copy-start(bf16[192,384]{1,0:T(8,128)(2,1)S(1)} %collective-permute-done.26.refs_17_.refs_22_) | copy-start | bytes 442372
  189.4 9.2 %copy-start.21 = (bf16[288,384]{1,0:T(8,128)(2,1)}, bf16[288,384]{1,0:T(8,128)(2,1)S(1)}, u32[]{:S(2)}) copy-start(bf16[288,384]{1,0:T(8,128)(2,1)S(1)} %collective-permute-done.25.refs_14_.refs_15_) | copy-start | bytes 663556
  201.9 9.6 %collective-permute-start.30 = (bf16[240,384]{1,0:T(8,128)(2,1)}, bf16[240,384]{1,0:T(8,128)(2,1)S(1)}, u32[]{:S(2)}, u32[]{:S(2)}) collective-permute-start(bf16[240,384]{1,0:T(8,128)(2,1)} %get-tuple-element.134.refs_9_), channel_id=1, source_target_pairs={{0,16},{2,18},{4,20},{6,22},{8,24},{10,26},{12,28},{14,30},{16,0},... | collective-permute-start | bytes 552968 | tf_op jit(solution)/shard_map/ppermute | solution.py:1063
  202.3 6.9 %collective-permute-start.31 = (bf16[192,384]{1,0:T(8,128)(2,1)}, bf16[192,384]{1,0:T(8,128)(2,1)S(1)}, u32[]{:S(2)}, u32[]{:S(2)}) collective-permute-start(bf16[192,384]{1,0:T(8,128)(2,1)} %get-tuple-element.135.refs_10_), channel_id=1, source_target_pairs={{0,8},{2,10},{4,12},{6,14},{8,0},{10,2},{12,4},{14,6},{16,24},{18,... | collective-permute-start | bytes 442376 | tf_op jit(solution)/shard_map/ppermute | solution.py:1063
  206.8 8.2 %collective-permute-start.29 = (bf16[160,384]{1,0:T(8,128)(2,1)}, bf16[160,384]{1,0:T(8,128)(2,1)S(1)}, u32[]{:S(2)}, u32[]{:S(2)}) collective-permute-start(bf16[160,384]{1,0:T(8,128)(2,1)} %get-tuple-element.137.own_ref), channel_id=1, source_target_pairs={{0,6},{2,4},{4,2},{6,0},{8,14},{10,12},{12,10},{14,8},{16,22},{18,... | collective-permute-start | bytes 368648 | tf_op jit(solution)/shard_map/ppermute | solution.py:1063
  206.9 8.1 %collective-permute-start.28 = (bf16[160,384]{1,0:T(8,128)(2,1)}, bf16[160,384]{1,0:T(8,128)(2,1)S(1)}, u32[]{:S(2)}, u32[]{:S(2)}) collective-permute-start(bf16[160,384]{1,0:T(8,128)(2,1)} %get-tuple-element.137.own_ref), channel_id=1, source_target_pairs={{0,2},{2,0},{4,6},{6,4},{8,10},{10,8},{12,14},{14,12},{16,18},{18,... | collective-permute-start | bytes 368648 | tf_op jit(solution)/shard_map/ppermute | solution.py:1063
  209.2 6.2 %collective-permute-start.27 = (bf16[160,384]{1,0:T(8,128)(2,1)}, bf16[160,384]{1,0:T(8,128)(2,1)S(1)}, u32[]{:S(2)}, u32[]{:S(2)}) collective-permute-start(bf16[160,384]{1,0:T(8,128)(2,1)} %get-tuple-element.137.own_ref), channel_id=1, source_target_pairs={{0,4},{2,6},{4,0},{6,2},{8,12},{10,14},{12,8},{14,10},{16,20},{18,... | collective-permute-start | bytes 368648 | tf_op jit(solution)/shard_map/ppermute | solution.py:1063
  209.2 2.3 %copy-start.27 = (bf16[192,384]{1,0:T(8,128)(2,1)}, bf16[192,384]{1,0:T(8,128)(2,1)S(1)}, u32[]{:S(2)}) copy-start(bf16[192,384]{1,0:T(8,128)(2,1)S(1)} %collective-permute-done.31.refs_17_) | copy-start | bytes 442372
  (15 other events, 12.1 us)
where the time goes:
time: 219 us; the launch traced here: 218 us
  Pallas kernels  146 us (67%)
  starting transfers between devices  30.7 us (14%)
  waiting for transfers between devices  28.8 us (13%)
  local copies, waits for them, and re-layouts  9.91 us (5%)
    pallas_call x19, Pallas kernels, call(): pl.pallas_call(body, out_shape=tuple(outs), in_specs=[VMEM] * vmem_in + [...  146 us
    ppermute x24, starting transfers between devices, swap(): return lax.ppermute(array, 'dp', [(d, d ^ flip) for d in range(self.count)])  20.4 us
    ppermute x24, waiting for transfers between devices, swap(): return lax.ppermute(array, 'dp', [(d, d ^ flip) for d in range(self.count)])  20.3 us
    unnamed x62, local copies, waits for them, and re-layouts  9.12 us
    ppermute x7, starting transfers between devices, swap(): return lax.ppermute(array, 'band', [(0, 1), (1, 0)])  8.88 us
    ppermute x7, waiting for transfers between devices, swap(): return lax.ppermute(array, 'band', [(0, 1), (1, 0)])  8.46 us
  transfers between devices with their start and end apart: 32, of which 12 were waited for; matrix products, arithmetic and copies ran while one was open for 1% of the time, Pallas kernels for 46%

commit v1 on v0

--- a/solution.py
+++ b/solution.py
@@ -26,6 +26,7 @@
     "attention_back": 18,
     "embed_back": 14,
     "combine": 12,
+    "mlp_out": 8,
     "touch": 20,
     "assemble": 0.5,
     "finish": 0.5,
@@ -125,7 +126,7 @@
         there, here = pl.ds(self.base + 2 * i, 2), pl.ds(2 * i, 2)
         return pltpu.make_async_copy(self.hbm.at[there], self.ref.at[here], self.sems.at[i])
 
-    def pick(self, seen_ref, out_ref):
+    def pick(self, seen_ref, out_ref, looped=True):
         wide = 2 * seen_ref.shape[1]
 
         def pair(i, carry):
@@ -136,40 +137,33 @@
             ).astype(BF)
             return carry
 
-        lax.fori_loop(0, self.pairs, pair, 0)
-
-
-def pick_far_kernel(
-    links, pairs, seen_ref, pixel_hbm, halves_hbm, half_hbm, out_hbm, pixel_ref, out_ref, half_ref, pixel_sems, sems
-):
+        if looped:
+            lax.fori_loop(0, self.pairs, pair, 0)
+        else:
+            for i in range(self.pairs):
+                pair(i, 0)
+
+
+def pick_far_kernel(links, pairs, seen_ref, pixel_hbm, out_hbm, pixel_ref, out_ref, pixel_sems, sems):
+    base = (1 - links.bit("band")) * 2 * pairs
+    Pixels(pixel_hbm, pixel_ref, base, pairs, pixel_sems).pick(seen_ref, out_ref, False)
     copies = Copies(sems)
-    base = (1 - links.bit("band")) * 2 * pairs
-    half_in = copies.start(halves_hbm.at[links.bit(0)], half_ref)
-    pixels = Pixels(pixel_hbm, pixel_ref, base, pairs, pixel_sems)
-    half_in.wait()
-    copies.out(half_ref, half_hbm)
-    pixels.pick(seen_ref, out_ref)
     copies.out(out_ref, out_hbm)
     copies.finish()
 
 
-def pick_far(links, seen, pixel_rows, halves):
+def pick_far(links, seen, pixel_rows):
     chips, depth, patches = pixel_rows.shape
     pairs = chips // 4
-    outs = (shape(halves.shape[1:], BF), shape((depth, chips // 2 * seen.shape[1]), BF))
+    out = shape((depth, chips // 2 * seen.shape[1]), BF)
     return kernel_call(
         functools.partial(pick_far_kernel, links, pairs),
         "pick_far",
-        outs,
-        (
-            shape((2 * pairs, depth, patches), BF),
-            outs[1],
-            outs[0],
-            pltpu.SemaphoreType.DMA((pairs,)),
-        ),
-        4,
+        (out,),
+        (shape((2 * pairs, depth, patches), BF), out, pltpu.SemaphoreType.DMA((pairs,))),
+        1,
         vmem_in=1,
-    )(seen, pixel_rows, halves)
+    )(seen, pixel_rows)[0]
 
 
 def prepare_kernel(
@@ -585,10 +579,8 @@
     vecs_ref,
     n2_hbm,
     gact_hbm,
-    act1_hbm,
     gpre1_hbm,
     up_hbm,
-    down_hbm,
     mid_hbm,
     cot_hbm,
     att_hbm,
@@ -596,23 +588,20 @@
     *rest,
 ):
     rest = rest[after:]
-    sends, (keep_hbm, branch_hbm, gatt_hbm, out_hbm, vec_ref) = rest[:3], rest[3:8]
+    sends, (keep_hbm, branch_hbm, gatt_hbm, act2_hbm, vec_ref) = rest[:3], rest[3:8]
     (
         n2_ref,
         gatt_ref,
-        out_ref,
-        act_ref,
         gpre_ref,
         up_ref,
-        down_ref,
         mid_ref,
         att_ref,
         wout_ref,
         back_ref,
         branch_ref,
         full_ref,
-    ) = rest[8:21]
-    half_refs, sems = rest[21:-1], rest[-1]
+    ) = rest[8:18]
+    half_refs, sems = rest[18:-1], rest[-1]
     copies = Copies(sems)
     rows, width = mid_ref.shape
     quarter = up_hbm.shape[1] // 4
@@ -639,11 +628,7 @@
         (sends[1], keep_hbm.at[middle:end, :]),
         more,
     )
-    late = [copies.start(act1_hbm, act_ref)] + [
-        copies.start(down_hbm.at[at(2 * i + third), :], down_ref.at[at(2 * third + i), :])
-        for third in range(2)
-        for i in range(2)
-    ]
+    copies.out(half.act, act2_hbm)
     for copy in first_in:
         copy.wait()
 
@@ -685,22 +670,10 @@
 
     tiles(width, attended_grad, LOOP[4])
     copies.out(gatt_ref, gatt_hbm)
-    for copy in late:
-        copy.wait()
-
-    def outward(cols):
-        out_ref[:, cols] = (
-            mid_ref[:, cols]
-            + dot(act_ref[...], down_ref[: 2 * quarter, cols])
-            + dot(half.act[...], down_ref[2 * quarter :, cols])
-        ).astype(BF)
-
-    tiles(width, outward, LOOP[3])
-    copies.out(out_ref, out_hbm)
     copies.finish()
 
 
-def mlp_back(links, vecs, n2, gact, act1, gpre1, up, down, mid, cot, att, wout, after):
+def mlp_back(links, vecs, n2, gact, gpre1, up, mid, cot, att, wout, after):
     rows, width = mid.shape
     hidden = up.shape[1]
     sums = shape((3 * width + hidden // 2, width // 2), BF)
@@ -708,14 +681,65 @@
         functools.partial(mlp_back_kernel, links, len(after)),
         "mlp_back",
         tuple(shape((count, width // 2), BF) for count in (2 * width, hidden // 2, width))
-        + (sums, cot, cot, cot, shape((2, width), F32)),
-        (n2, cot, cot, act1, gpre1)
-        + (shape((width, hidden // 2), BF), down, mid, att, wout, mid, cot, wout)
+        + (sums, cot, cot, gpre1, shape((2, width), F32)),
+        (n2, cot, gpre1)
+        + (shape((width, hidden // 2), BF), mid, att, wout, mid, cot, wout)
         + MlpHalf.scratch(rows, width, hidden),
         140,
         vmem_in=1,
         vmem_out=1,
-    )(vecs, n2, gact, act1, gpre1, up, down, mid, cot, att, wout, *after)
+    )(vecs, n2, gact, gpre1, up, mid, cot, att, wout, *after)
+
+
+def mlp_out_kernel(chips, after, act1_hbm, act2_hbm, down_hbm, mid_hbm, *rest):
+    out_hbm = rest[after]
+    act1_ref, act2_ref, down_ref, mid_ref, rows_ref, out_ref, sems = rest[after + 1 :]
+    copies = Copies(sems)
+    rows, width = mid_ref.shape
+    slots = (rows - TAIL) // chips
+    quarter = down_hbm.shape[0] // 4
+    at = lambda i: slice(i * quarter, (i + 1) * quarter)
+    arrive = []
+    for third, source, target in ((0, act1_hbm, act1_ref), (1, act2_hbm, act2_ref)):
+        arrive.append(copies.start(source, target))
+        for i in range(2):
+            arrive.append(
+                copies.start(down_hbm.at[at(2 * i + third), :], down_ref.at[at(2 * third + i), :])
+            )
+    arrive.append(copies.start(mid_hbm, mid_ref))
+    for copy in arrive:
+        copy.wait()
+
+    def outward(cols):
+        rows_ref[:, cols] = (
+            mid_ref[:, cols]
+            + dot(act1_ref[...], down_ref[: 2 * quarter, cols])
+            + dot(act2_ref[...], down_ref[2 * quarter :, cols])
+        )
+
+    tiles(width, outward, True)
+
+    def chip(c, carry):
+        first = rows_ref[pl.ds(rows - TAIL + c, 1), :]
+        others = rows_ref[pl.ds(pl.multiple_of(c * slots, slots), slots), :]
+        out_ref[c] = jnp.concatenate([first, others], axis=0).astype(BF)
+        return carry
+
+    lax.fori_loop(0, chips, chip, 0)
+    copies.out(out_ref, out_hbm)
+    copies.finish()
+
+
+def mlp_out(chips, act1, act2, down, mid, after):
+    rows, width = mid.shape
+    out = shape((chips, (rows - TAIL) // chips + 1, width), BF)
+    return kernel_call(
+        functools.partial(mlp_out_kernel, chips, len(after)),
+        "mlp_out",
+        (out,),
+        (act1, act2, down, mid, mid, out),
+        8,
+    )(act1, act2, down, mid, *after)[0]
 
 
 def split_vec(vec):
@@ -1485,13 +1509,11 @@
 
     pixel_rows = jnp.swapaxes(pixels, 2, 3).reshape(group_chips, depth, patches)
     kernels_own = kernels.reshape(depth, width)
-    my_half, picked_far = pick_far(
-        links, visible, pixel_rows, kernels_own.reshape(2, depth // 2, width)
-    )
+    my_half = lax.dynamic_slice_in_dim(kernels_own, links.bit(0) * (depth // 2), depth // 2, 0)
     far_half = links.swap(my_half, "band")
-    picked_in = links.swap(picked_far, "band")
+    picked_in = links.swap(pick_far(links, visible, pixel_rows), "band")
+    far_half, cotangent = lax.optimization_barrier((far_half, cotangent))
     picked_own, cot, gact = prepare(links, visible, pixel_rows, cotangent, mlp_down)
-    far_half, cot = lax.optimization_barrier((far_half, cot))
     far_other = links.swap(far_half, 0)
     vecs = jnp.stack(
         [class_token, norm1_gain, norm1_bias, norm2_gain, norm2_bias] + [class_token] * 3
@@ -1525,8 +1547,8 @@
     up1 = Piece(
         (3, 1, 0, "band"), (2,) * 4, 4 * block, [(up_keep, 0), (links.bring(up_send, "band"), 0)], y
     )
-    *sums_send, sums_keep, branch, gatt, out_rows, vec2 = mlp_back(
-        links, vecs, n2, gact, act1, gpre1, mlp_up, mlp_down, mid, cot, att, attn_out, ()
+    *sums_send, sums_keep, branch, gatt, act2, vec2 = mlp_back(
+        links, vecs, n2, gact, gpre1, mlp_up, mid, cot, att, attn_out, ()
     )
     both = lambda i, at: [(sums_keep, at), (links.bring(sums_send[i], 0), 0)]
     middle, end = 2 * width, 2 * width + mlp_up.shape[1] // 2
@@ -1534,13 +1556,6 @@
     up2 = Piece((0, 3, 1, "band"), (2,) * 4, 4 * block, both(1, middle), core)
     names, sizes = (0, 1, "band", 3, 2), (2,) * 5
     outp = Piece(names, sizes, block, both(2, end), core)
-    block_output = jnp.concatenate(
-        [
-            out_rows[body : body + chips][:, None, :],
-            out_rows[:body].reshape(chips, slots, width),
-        ],
-        axis=1,
-    )
     tie, unused = combine(links, [(down1, core, "split"), (up1, core, "split")], (vec2,))
     tie, unused = combine(
         links,
@@ -1551,7 +1566,7 @@
             (up2, y, "split"),
             (outp, (2,), "split"),
         ],
-        (*tie, block_output),
+        tie,
     )
 
     gpacked, qkv_send, qkv_keep = attention_back(links, chips, gatt, packed, probs, tprobs, n1, tie)
@@ -1622,6 +1637,7 @@
         ],
         (partly,),
     )
+    block_output = mlp_out(chips, act1, act2, mlp_down, mid, tie)
     scattered = scatter(links, 1, far_grads, depth, visible, patches, partly)
     pixel_grads = jnp.swapaxes(scattered.reshape(group_chips, bands, pix, patches), 2, 3)
     tie, unused = combine(
@@ -1632,7 +1648,7 @@
             (up, (2,), "split"),
             (down2, (3,), "split"),
         ],
-        (scattered,),
+        (scattered, block_output),
     )
     tie, (kgrad,) = combine(links, [(kg, BF, "final"), (vec, (), "vec")], tie, "finish")
     vec_sum = links.total(vec.value())

time: 219 us -> 215 us (0.982)
  waiting for transfers between devices: 28.8 us -> 16.3 us
  Pallas kernels: 146 us -> 151 us
  starting transfers between devices: 30.7 us -> 34.2 us
    ppermute x24, waiting for transfers between devices: 20.3 us -> 8.03 us  [swap(): return lax.ppermute(array, 'dp', [(d, d ^ flip) for d in range(self.count)])]
    pallas_call x19 -> x20, Pallas kernels: 146 us -> 151 us  [call(): pl.pallas_call(body, out_shape=tuple(outs), in_specs=[VMEM] * vmem_in + [...]
    ppermute x7, waiting for transfers between devices: 8.46 us -> 3.75 us  [swap(): return lax.ppermute(array, 'band', [(0, 1), (1, 0)])]
    ppermute x1, waiting for transfers between devices: 0.01 us -> 4.51 us  [swap(): return lax.ppermute(array, ('dp', 'band'), pairs)]
    ppermute x24, starting transfers between devices: 20.4 us -> 24.4 us  [swap(): return lax.ppermute(array, 'dp', [(d, d ^ flip) for d in range(self.count)])]
    unnamed x62 -> x60, local copies, waits for them, and re-layouts: 9.12 us -> 8.94 us
  transfers between devices with their start and end apart: 32 -> 32, of which waited for: 12 -> 12; matrix products, arithmetic and copies ran while one was open for 1% -> 0% of each run, Pallas kernels for 46% -> 50%
where the time goes in v1:
time: 215 us; the launch traced here: 214 us
  Pallas kernels  151 us (70%)
  starting transfers between devices  34.2 us (16%)
  waiting for transfers between devices  16.3 us (8%)
  local copies, waits for them, and re-layouts  10.6 us (5%)
    pallas_call x20, Pallas kernels, call(): pl.pallas_call(body, out_shape=tuple(outs), in_specs=[VMEM] * vmem_in + [...  151 us
    ppermute x24, starting transfers between devices, swap(): return lax.ppermute(array, 'dp', [(d, d ^ flip) for d in range(self.count)])  24.4 us
    unnamed x60, local copies, waits for them, and re-layouts  8.94 us
    ppermute x24, waiting for transfers between devices, swap(): return lax.ppermute(array, 'dp', [(d, d ^ flip) for d in range(self.count)])  8.03 us
    ppermute x7, starting transfers between devices, swap(): return lax.ppermute(array, 'band', [(0, 1), (1, 0)])  7.47 us
    ppermute x1, waiting for transfers between devices, swap(): return lax.ppermute(array, ('dp', 'band'), pairs)  4.51 us
  transfers between devices with their start and end apart: 32, of which 12 were waited for; matrix products, arithmetic and copies ran while one was open for 0% of the time, Pallas kernels for 50%

profile of v1, /device:TPU:0, one launch (start us, length us, event | category | flops | bytes accessed | tf_op | source)
XLA Modules:
  0.0 213.9 jit_solution(10621433690860089015)
XLA Ops:
  0.7 1.0 constant_dynamic-slice_fusion
  1.6 3.0 %collective-permute-start = (bf16[160,768]{1,0:T(8,128)(2,1)S(1)}, bf16[160,768]{1,0:T(8,128)(2,1)S(1)}, u32[]{:S(2)}, u32[]{:S(2)}) collective-permute-start(bf16[160,768]{1,0:T(8,128)(2,1)S(1)} %constant_dynamic-slice_fusion), channel_id=1, source_target_pairs={{0,1},{1,0},{2,3},{3,2},{4,5},{5,4},{6,7},{7,6},{8,9},{9,8},{10,11... | collective-permute-start | bytes 737288 | tf_op jit(solution)/shard_map/ppermute | solution.py:1089
  4.7 4.4 %pick_far.1 = bf16[320,768]{1,0:T(8,128)(2,1)} custom-call(s32[24,64]{1,0:T(8,128)} %seen_ref.7, bf16[24,320,256]{2,1,0:T(8,128)(2,1)} %bitcast.17), custom_call_target="tpu_custom_call" | custom-call | flops 5750000128 | bytes 1 | tf_op jit(solution)/shard_map/pick_far/pallas_call | solution.py:51
  10.6 12.1 %prepare.1 = (bf16[320,768]{1,0:T(8,128)(2,1)}, bf16[784,768]{1,0:T(8,128)(2,1)}, bf16[784,3072]{1,0:T(8,128)(2,1)}) custom-call(s32[24,64]{1,0:T(8,128)} %seen_ref.7, bf16[24,320,256]{2,1,0:T(8,128)(2,1)} %bitcast.18, bf16[12,65,768]{2,1,0:T(8,128)(2,1)} %cot_hbm, bf16[3072,768]{1,0:T(8,128)(2,1)} %down_hbm.3), custom_call_target="tpu_custom_call" | custom-call | flops 12650000384 | bytes 1 | tf_op jit(solution)/shard_map/prepare/pallas_call | solution.py:51
  23.6 31.8 %encoder_forward.1 = (f32[784,768]{1,0:T(8,128)}, bf16[784,768]{1,0:T(8,128)(2,1)}, bf16[784,2304]{1,0:T(8,128)(2,1)}, bf16[12,6,80,128]{3,2,1,0:T(8,128)(2,1)},...) custom-call(f32[8,768]{1,0:T(8,128)} %stack.26.vecs_ref, ...), custom_call_target="tpu_custom_call" | custom-call | flops 35649998848 | bytes 1 | tf_op jit(solution)/shard_map/encoder_forward/pallas_call | solution.py:51
  55.3 1.8 collective-permute-start.3
  57.1 1.7 collective-permute-start.4
  58.8 24.2 %mlp_back.1 = (bf16[1536,384]{1,0:T(8,128)(2,1)}, bf16[1536,384]{1,0:T(8,128)(2,1)}, bf16[768,384]{1,0:T(8,128)(2,1)}, bf16[3840,384]{1,0:T(8,128)(2,1)}, bf16[7...) custom-call(f32[8,768]{1,0:T(8,128)} %stack.26.vecs_ref, ...), custom_call_target="tpu_custom_call" | custom-call | flops 36800000000 | bytes 1 | tf_op jit(solution)/shard_map/mlp_back/pallas_call | solution.py:51
  84.0 1.6 collective-permute-done.4.refs_3_.refs_4_.refs_11_.refs_10_
  85.5 2.7 %combine.7.refs_9_ = bf16[1536,384]{1,0:T(8,128)(2,1)} custom-call(bf16[1536,384]{1,0:T(8,128)(2,1)} %get-tuple-element.94.refs_0_.refs_7_.refs_15_.refs_18_, bf16[1536,384]{1,0:T(8,128)(2,1)} %copy-done.13, bf16[1536,384]{1,0:T(8,128)(2,1)} %get-tuple-element.96.refs_2_.refs_3_.refs_10_.refs_8_.refs_9_, ...), custom_call_target="tpu_custom_call" | custom-call | flops 13799999488 | bytes 1 | tf_op jit(solution)/shard_map/combine/pallas_call | solution.py:51
  88.8 3.4 %collective-permute-done.8.refs_8_.refs_12_.refs_11_ = bf16[768,384]{1,0:T(8,128)(2,1)S(1)} collective-permute-done((bf16[768,384]{1,0:T(8,128)(2,1)}, bf16[768,384]{1,0:T(8,128)(2,1)S(1)}, u32[]{:S(2)}, u32[]{:S(2)}) %collective-permute-start.8) | collective-permute-done | bytes 589856 | tf_op jit(solution)/shard_map/ppermute | solution.py:1087
  92.2 0.8 copy-done.16
  93.5 3.6 %combine.8 = (bf16[1152,384]{1,0:T(8,128)(2,1)}, bf16[1152,384]{1,0:T(8,128)(2,1)}, bf16[384,384]{1,0:T(8,128)(2,1)}) custom-call(bf16[1536,384]{1,0:T(8,128)(2,1)} %get-tuple-element.94.refs_0_.refs_7_.refs_15_.refs_18_, bf16[1536,384]{1,0:T(8,128)(2,1)} %copy-done.13, bf16[1536,384]{1,0:T(8,128)(2,1)} %copy-done.14, ...), custom_call_target="tpu_custom_call" | custom-call | flops 13799999488 | bytes 1 | tf_op jit(solution)/shard_map/combine/pallas_call | solution.py:51
  97.0 1.3 collective-permute-start.10
  98.3 1.7 collective-permute-start.11
  100.0 1.6 collective-permute-start.12
  101.6 17.9 %attention_back.1 = (bf16[784,2304]{1,0:T(8,128)(2,1)}, bf16[2304,384]{1,0:T(8,128)(2,1)}, bf16[2304,384]{1,0:T(8,128)(2,1)}) custom-call(bf16[784,768]{1,0:T(8,128)(2,1)} %get-tuple-element.89.gatt_hbm, bf16[784,2304]{1,0:T(8,128)(2,1)} %get-tuple-element.90.packed_hbm, bf16[12,6,80,128]{3,2,1,0:T(8,128)(2,1)} %get-tuple-element.91.probs_hbm, ...), custom_call_target="tpu_custom_call" | custom-call | flops 20700000256 | bytes 1 | tf_op jit(solution)/shard_map/attention_back/pallas_call | solution.py:51
  120.0 1.3 touch.2.refs_14_
  121.3 2.2 %collective-permute-done.9.refs_6_.refs_4_.refs_1_ = bf16[2304,384]{1,0:T(8,128)(2,1)S(1)} collective-permute-done((bf16[2304,384]{1,0:T(8,128)(2,1)}, bf16[2304,384]{1,0:T(8,128)(2,1)S(1)}, u32[]{:S(2)}, u32[]{:S(2)}) %collective-permute-start.9) | collective-permute-done | bytes 1769504 | tf_op jit(solution)/shard_map/ppermute | solution.py:1087
  123.5 1.2 copy-done.12
  124.7 3.7 %combine.9 = (bf16[896,384]{1,0:T(8,128)(2,1)}, bf16[1024,384]{1,0:T(8,128)(2,1)}, bf16[192,384]{1,0:T(8,128)(2,1)}, bf16[384,384]{1,0:T(8,128)(2,1)}) custom-call(bf16[3840,384]{1,0:T(8,128)(2,1)} %get-tuple-element.99.refs_5_.refs_0_.refs_7_.refs_10_.refs_8_, bf16[1536,384]{1,0:T(8,128)(2,1)} %collective-permute-done.6.refs_6_.refs_1_.refs_11_.refs_16_.refs_21_, ...), custom_call_target="tpu_custom_call" | custom-call | flops 13799999488 | bytes 1 | tf_op jit(solution)/shard_map/combine/pallas_call | solution.py:51
  128.5 0.9 collective-permute-start.13
  129.6 2.6 %collective-permute-start.16 = (bf16[384,384]{1,0:T(8,128)(2,1)}, bf16[384,384]{1,0:T(8,128)(2,1)S(1)}, u32[]{:S(2)}, u32[]{:S(2)}) collective-permute-start(bf16[384,384]{1,0:T(8,128)(2,1)} %get-tuple-element.114.rest_3_), channel_id=1, source_target_pairs={{0,16},{2,18},{4,20},{6,22},{8,24},{10,26},{12,28},{14,30},{16,0},... | collective-permute-start | bytes 884744 | tf_op jit(solution)/shard_map/ppermute | solution.py:1087
  132.2 0.9 collective-permute-start.17
  133.1 13.3 %embed_back.1 = (bf16[672,384]{1,0:T(8,128)(2,1)}, bf16[640,384]{1,0:T(8,128)(2,1)}, bf16[2,320,384]{2,1,0:T(8,128)(2,1)}, bf16[2,320,384]{2,1,0:T(8,128)(2,1)}, f32[16,384]{1,0:T(8,128)}) custom-call(f32[8,768]{1,0:T(8,128)} %stack.26.vecs_ref, f32[2,768]{1,0:T(2,128)} %get-tuple-element.98.refs_4_.vec2_ref, ...), custom_call_target="tpu_custom_call" | custom-call | flops 16099999744 | bytes 1 | tf_op jit(solution)/shard_map/embed_back/pallas_call | solution.py:51
  146.9 1.5 collective-permute-done.13.refs_1_.refs_5_.refs_2_
  148.3 0.9 copy-done.15
  149.2 1.3 touch.3.refs_19_
  150.6 0.8 copy-done
  151.4 3.7 %combine.10 = (bf16[496,384]{1,0:T(8,128)(2,1)}, bf16[560,384]{1,0:T(8,128)(2,1)}, bf16[240,384]{1,0:T(8,128)(2,1)}, f32[16,384]{1,0:T(8,128)}, bf16[192,384]{1,0:T(8,128)(2,1)}, /*index=5*/bf16[288,384]{1,0:T(8,128)(2,1)}) custom-call(bf16[640,384]{1,0:T(8,128)(2,1)} %get-tuple-element.115.refs_0_.refs_6_, bf16[672,384]{1,0:T(8,128)(2,1)} %copy-done, ...), custom_call_target="tpu_custom_call" | custom-call | flops 13799999488 | bytes 1 | tf_op jit(solution)/shard_map/combine/pallas_call | solution.py:51
  155.4 0.8 collective-permute-start.19
  156.3 2.4 %collective-permute-start.20 = (bf16[240,384]{1,0:T(8,128)(2,1)}, bf16[240,384]{1,0:T(8,128)(2,1)S(1)}, u32[]{:S(2)}, u32[]{:S(2)}) collective-permute-start(bf16[240,384]{1,0:T(8,128)(2,1)} %get-tuple-element.120), channel_id=1, source_target_pairs={{0,5},{1,4},{2,7},{3,6},{4,1},{5,0},{6,3},{7,2},{8,13},{9,12},{10,... | collective-permute-start | bytes 552968 | tf_op jit(solution)/shard_map/ppermute | solution.py:1093
  158.6 4.6 %scatter.2.refs_14_.rest_0_ = f32[24,320,256]{2,1,0:T(8,128)} custom-call(s32[24,64]{1,0:T(8,128)} %seen_ref.7, bf16[640,384]{1,0:T(8,128)(2,1)} %bitcast.22), custom_call_target="tpu_custom_call" | custom-call | flops 4600000000 | bytes 1 | tf_op jit(solution)/shard_map/scatter/pallas_call | solution.py:51
  163.6 2.6 %collective-permute-start.25 = (bf16[288,384]{1,0:T(8,128)(2,1)}, bf16[288,384]{1,0:T(8,128)(2,1)}, u32[]{:S(2)}, u32[]{:S(2)}) collective-permute-start(bf16[288,384]{1,0:T(8,128)(2,1)} %get-tuple-element.128), channel_id=1, source_target_pairs={{0,16},{2,18},{4,20},{6,22},{8,24},{10,26},{12,28},{14,30},{16,0},... | collective-permute-start | bytes 663560 | tf_op jit(solution)/shard_map/ppermute | solution.py:1087
  166.2 4.5 %collective-permute-done.20.refs_8_.refs_4_ = bf16[240,384]{1,0:T(8,128)(2,1)S(1)} collective-permute-done((bf16[240,384]{1,0:T(8,128)(2,1)}, bf16[240,384]{1,0:T(8,128)(2,1)S(1)}, u32[]{:S(2)}, u32[]{:S(2)}) %collective-permute-start.20) | collective-permute-done | bytes 184352 | tf_op jit(solution)/shard_map/ppermute | solution.py:1093
  172.9 2.7 %combine.11 = (bf16[480,384]{1,0:T(8,128)(2,1)}, bf16[192,384]{1,0:T(8,128)(2,1)}, bf16[192,384]{1,0:T(8,128)(2,1)}, f32[16,384]{1,0:T(8,128)}, f32[48,384]{1,0:T(8,128)}) custom-call(bf16[2304,384]{1,0:T(8,128)(2,1)} %get-tuple-element.106.refs_5_.refs_3_.refs_0_, bf16[2304,384]{1,0:T(8,128)(2,1)} %copy-done.12, bf16[1024,384]{1,0:T(8,128)(2,1)} %copy-done.15, ...), custom_call_target="tpu_custom_call" | custom-call | flops 13799999488 | bytes 1 | tf_op jit(solution)/shard_map/combine/pallas_call | solution.py:51
  176.3 2.6 %collective-permute-start.23 = (bf16[192,384]{1,0:T(8,128)(2,1)}, bf16[192,384]{1,0:T(8,128)(2,1)S(1)}, u32[]{:S(2)}, u32[]{:S(2)}) collective-permute-start(bf16[192,384]{1,0:T(8,128)(2,1)} %get-tuple-element.124.rest_1_), channel_id=1, source_target_pairs={{0,16},{2,18},{4,20},{6,22},{8,24},{10,26},{12,28},{14,30},{16,0},... | collective-permute-start | bytes 442376 | tf_op jit(solution)/shard_map/ppermute | solution.py:1087
  178.9 10.2 %mlp_out.1.refs_19_ = bf16[12,65,768]{2,1,0:T(8,128)(2,1)} custom-call(bf16[784,1536]{1,0:T(8,128)(2,1)} %get-tuple-element.83.act1_hbm, bf16[784,1536]{1,0:T(8,128)(2,1)} %get-tuple-element.88.act2_hbm, bf16[3072,768]{1,0:T(8,128)(2,1)} %down_hbm.3, f32[784,768]{1,0:T(8,128)} %get-tuple-element.86.mid_hbm, bf16[480,384]{1,0:T(8,128)(2,1)} %get-tuple-element.123.rest_0_, ...), custom_call_target="tpu_custom_call" | custom-call | flops 9200000000 | bytes 1 | tf_op jit(solution)/shard_map/mlp_out/pallas_call | solution.py:51
  189.1 1.2 collective-permute-start.24
  190.3 4.5 %scatter.3.refs_18_.refs_23_ = f32[24,320,256]{2,1,0:T(8,128)} custom-call(s32[24,64]{1,0:T(8,128)} %seen_ref.7, bf16[640,384]{1,0:T(8,128)(2,1)} %copy-done.19, f32[24,320,256]{2,1,0:T(8,128)} %scatter.2.refs_14_.rest_0_), custom_call_target="tpu_custom_call", output_to_operand_aliasing={{}: (2, {})} | custom-call | flops 4600000000 | bytes 1 | tf_op jit(solution)/shard_map/scatter/pallas_call | solution.py:51
  195.6 2.4 %combine.12 = (bf16[240,384]{1,0:T(8,128)(2,1)}, bf16[192,384]{1,0:T(8,128)(2,1)}) custom-call(bf16[2304,384]{1,0:T(8,128)(2,1)} %get-tuple-element.106.refs_5_.refs_3_.refs_0_, bf16[2304,384]{1,0:T(8,128)(2,1)} %copy-done.12, bf16[1024,384]{1,0:T(8,128)(2,1)} %copy-done.15, bf16[560,384]{1,0:T(8,128)(2,1)} %copy-done.1, bf16[480,384]{1,0:T(8,128)(2,1)} %copy-done.3, ...), custom_call_target="tpu_custom_call" | custom-call | flops 13799999488 | bytes 1 | tf_op jit(solution)/shard_map/combine/pallas_call | solution.py:51
  198.0 1.7 collective-permute-start.30
  199.8 1.6 collective-permute-start.31
  202.1 2.2 %finish.1 = (bf16[160,384]{1,0:T(8,128)(2,1)}, f32[16,384]{1,0:T(8,128)}) custom-call(bf16[640,384]{1,0:T(8,128)(2,1)} %get-tuple-element.115.refs_0_.refs_6_, bf16[672,384]{1,0:T(8,128)(2,1)} %copy-done, bf16[496,384]{1,0:T(8,128)(2,1)} %copy-done.2, bf16[560,384]{1,0:T(8,128)(2,1)} %copy-done.1, bf16[240,384]{1,0:T(8,128)(2,1)} %copy-done.4, ...), custom_call_target="tpu_custom_call" | custom-call | flops 575000000 | bytes 1 | tf_op jit(solution)/shard_map/finish/pallas_call | solution.py:51
  204.3 0.9 collective-permute-start.27
  205.1 1.3 collective-permute-start.29
  207.8 2.8 %combine.13 = (f32[144,384]{1,0:T(8,128)}, f32[192,384]{1,0:T(8,128)}, f32[48,1536]{1,0:T(8,128)}) custom-call(bf16[2304,384]{1,0:T(8,128)(2,1)} %get-tuple-element.106.refs_5_.refs_3_.refs_0_, bf16[2304,384]{1,0:T(8,128)(2,1)} %copy-done.12, bf16[1024,384]{1,0:T(8,128)(2,1)} %copy-done.15, bf16[560,384]{1,0:T(8,128)(2,1)} %copy-done.1, ...), custom_call_target="tpu_custom_call" | custom-call | flops 13799999488 | bytes 1 | tf_op jit(solution)/shard_map/combine/pallas_call | solution.py:51
  211.6 2.1 assemble.1
  (103 shorter events, 12.8 us)
Async XLA Ops:
  1.6 9.0 %collective-permute-start = (bf16[160,768]{1,0:T(8,128)(2,1)S(1)}, bf16[160,768]{1,0:T(8,128)(2,1)S(1)}, u32[]{:S(2)}, u32[]{:S(2)}) collective-permute-start(bf16[160,768]{1,0:T(8,128)(2,1)S(1)} %constant_dynamic-slice_fusion), channel_id=1, source_target_pairs={{0,1},{1,0},{2,3},{3,2},{4,5},{5,4},{6,7},{7,6},{8,9},{9,8},{10,11... | collective-permute-start | bytes 737288 | tf_op jit(solution)/shard_map/ppermute | solution.py:1089
  4.7 4.6 %copy-start.7 = (f32[768]{0:T(1024)S(1)}, f32[768]{0:T(1024)}, u32[]{:S(2)}) copy-start(f32[768]{0:T(1024)} %param.16) | copy-start | bytes 9220
  4.7 4.6 %copy-start.8 = (f32[768]{0:T(1024)S(1)}, f32[768]{0:T(1024)}, u32[]{:S(2)}) copy-start(f32[768]{0:T(1024)} %param.17) | copy-start | bytes 9220
  4.7 4.6 %copy-start.9 = (f32[768]{0:T(1024)S(1)}, f32[768]{0:T(1024)}, u32[]{:S(2)}) copy-start(f32[768]{0:T(1024)} %param.18) | copy-start | bytes 9220
  4.7 4.6 %copy-start.10 = (f32[768]{0:T(1024)S(1)}, f32[768]{0:T(1024)}, u32[]{:S(2)}) copy-start(f32[768]{0:T(1024)} %param.19) | copy-start | bytes 9220
  4.7 4.6 %copy-start.11 = (f32[768]{0:T(1024)S(1)}, f32[768]{0:T(1024)}, u32[]{:S(2)}) copy-start(f32[768]{0:T(1024)} %param.20) | copy-start | bytes 9220
  9.1 13.6 %collective-permute-start.1 = (bf16[320,768]{1,0:T(8,128)(2,1)}, bf16[320,768]{1,0:T(8,128)(2,1)S(1)}, u32[]{:S(2)}, u32[]{:S(2)}) collective-permute-start(bf16[320,768]{1,0:T(8,128)(2,1)} %pick_far.1), channel_id=1, source_target_pairs={{0,1},{1,0},{2,3},{3,2},{4,5},{5,4},{6,7},{7,6},{8,9},{9,8},{10,11... | collective-permute-start | bytes 1474568 | tf_op jit(solution)/shard_map/ppermute | solution.py:1089
  10.6 12.1 %copy-start.21 = (bf16[160,768]{1,0:T(8,128)(2,1)}, bf16[160,768]{1,0:T(8,128)(2,1)S(1)}, u32[]{:S(2)}) copy-start(bf16[160,768]{1,0:T(8,128)(2,1)S(1)} %collective-permute-done.half_hbm) | copy-start | bytes 737284
  10.6 12.1 %collective-permute-start.2 = (bf16[160,768]{1,0:T(8,128)(2,1)S(1)}, bf16[160,768]{1,0:T(8,128)(2,1)S(1)}, u32[]{:S(2)}, u32[]{:S(2)}) collective-permute-start(bf16[160,768]{1,0:T(8,128)(2,1)S(1)} %collective-permute-done.half_hbm), channel_id=1, source_target_pairs={{0,2},{2,0},{4,6},{6,4},{8,10},{10,8},{12,14},{14,12},{16,18},{18,... | collective-permute-start | bytes 737288 | tf_op jit(solution)/shard_map/ppermute | solution.py:1087
  55.3 28.6 %collective-permute-start.3 = (bf16[1536,384]{1,0:T(8,128)(2,1)}, bf16[1536,384]{1,0:T(8,128)(2,1)S(1)}, u32[]{:S(2)}, u32[]{:S(2)}) collective-permute-start(bf16[1536,384]{1,0:T(8,128)(2,1)} %get-tuple-element.95), channel_id=1, source_target_pairs={{0,4},{2,6},{4,0},{6,2},{8,12},{10,14},{12,8},{14,10},{16,20},{18,... | collective-permute-start | bytes 3538952 | tf_op jit(solution)/shard_map/ppermute | solution.py:1087
  57.1 28.4 %collective-permute-start.4 = (bf16[1536,384]{1,0:T(8,128)(2,1)}, bf16[1536,384]{1,0:T(8,128)(2,1)}, u32[]{:S(2)}, u32[]{:S(2)}) collective-permute-start(bf16[1536,384]{1,0:T(8,128)(2,1)} %get-tuple-element.97), channel_id=1, source_target_pairs={{0,1},{1,0},{2,3},{3,2},{4,5},{5,4},{6,7},{7,6},{8,9},{9,8},{10,11... | collective-permute-start | bytes 3538952 | tf_op jit(solution)/shard_map/ppermute | solution.py:1089
  83.0 9.2 %collective-permute-start.6 = (bf16[1536,384]{1,0:T(8,128)(2,1)}, bf16[1536,384]{1,0:T(8,128)(2,1)}, u32[]{:S(2)}, u32[]{:S(2)}) collective-permute-start(bf16[1536,384]{1,0:T(8,128)(2,1)} %get-tuple-element.100), channel_id=1, source_target_pairs={{0,2},{2,0},{4,6},{6,4},{8,10},{10,8},{12,14},{14,12},{16,18},{18,... | collective-permute-start | bytes 3538952 | tf_op jit(solution)/shard_map/ppermute | solution.py:1087
  83.1 9.1 %collective-permute-start.7 = (bf16[1536,384]{1,0:T(8,128)(2,1)}, bf16[1536,384]{1,0:T(8,128)(2,1)}, u32[]{:S(2)}, u32[]{:S(2)}) collective-permute-start(bf16[1536,384]{1,0:T(8,128)(2,1)} %get-tuple-element.101), channel_id=1, source_target_pairs={{0,2},{2,0},{4,6},{6,4},{8,10},{10,8},{12,14},{14,12},{16,18},{18,... | collective-permute-start | bytes 3538952 | tf_op jit(solution)/shard_map/ppermute | solution.py:1087
  84.0 1.6 copy-start.13
  88.2 4.0 %collective-permute-start.5 = (bf16[1536,384]{1,0:T(8,128)(2,1)}, bf16[1536,384]{1,0:T(8,128)(2,1)S(1)}, u32[]{:S(2)}, u32[]{:S(2)}) collective-permute-start(bf16[1536,384]{1,0:T(8,128)(2,1)} %combine.7.refs_9_), channel_id=1, source_target_pairs={{0,2},{2,0},{4,6},{6,4},{8,10},{10,8},{12,14},{14,12},{16,18},{18,... | collective-permute-start | bytes 3538952 | tf_op jit(solution)/shard_map/ppermute | solution.py:1087
  88.3 3.9 %collective-permute-start.8 = (bf16[768,384]{1,0:T(8,128)(2,1)}, bf16[768,384]{1,0:T(8,128)(2,1)S(1)}, u32[]{:S(2)}, u32[]{:S(2)}) collective-permute-start(bf16[768,384]{1,0:T(8,128)(2,1)} %get-tuple-element.102), channel_id=1, source_target_pairs={{0,2},{2,0},{4,6},{6,4},{8,10},{10,8},{12,14},{14,12},{16,18},{18,... | collective-permute-start | bytes 1769480 | tf_op jit(solution)/shard_map/ppermute | solution.py:1087
  92.2 1.2 copy-start.14
  97.0 22.6 %collective-permute-start.10 = (bf16[1152,384]{1,0:T(8,128)(2,1)}, bf16[1152,384]{1,0:T(8,128)(2,1)}, u32[]{:S(2)}, u32[]{:S(2)}) collective-permute-start(bf16[1152,384]{1,0:T(8,128)(2,1)} %get-tuple-element.104.rest_1_), channel_id=1, source_target_pairs={{0,4},{2,6},{4,0},{6,2},{8,12},{10,14},{12,8},{14,10},{16,20},{18,... | collective-permute-start | bytes 2654216 | tf_op jit(solution)/shard_map/ppermute | solution.py:1087
  98.3 21.7 %collective-permute-start.11 = (bf16[1152,384]{1,0:T(8,128)(2,1)}, bf16[1152,384]{1,0:T(8,128)(2,1)}, u32[]{:S(2)}, u32[]{:S(2)}) collective-permute-start(bf16[1152,384]{1,0:T(8,128)(2,1)} %get-tuple-element.103.rest_0_), channel_id=1, source_target_pairs={{0,1},{1,0},{2,3},{3,2},{4,5},{5,4},{6,7},{7,6},{8,9},{9,8},{10,11... | collective-permute-start | bytes 2654216 | tf_op jit(solution)/shard_map/ppermute | solution.py:1089
  100.0 19.6 %collective-permute-start.12 = (bf16[384,384]{1,0:T(8,128)(2,1)}, bf16[384,384]{1,0:T(8,128)(2,1)}, u32[]{:S(2)}, u32[]{:S(2)}) collective-permute-start(bf16[384,384]{1,0:T(8,128)(2,1)} %get-tuple-element.105.rest_2_), channel_id=1, source_target_pairs={{0,8},{2,10},{4,12},{6,14},{8,0},{10,2},{12,4},{14,6},{16,24},{18,... | collective-permute-start | bytes 884744 | tf_op jit(solution)/shard_map/ppermute | solution.py:1087
  119.5 4.0 %collective-permute-start.9 = (bf16[2304,384]{1,0:T(8,128)(2,1)}, bf16[2304,384]{1,0:T(8,128)(2,1)S(1)}, u32[]{:S(2)}, u32[]{:S(2)}) collective-permute-start(bf16[2304,384]{1,0:T(8,128)(2,1)} %get-tuple-element.107), channel_id=1, source_target_pairs={{0,2},{2,0},{4,6},{6,4},{8,10},{10,8},{12,14},{14,12},{16,18},{18,... | collective-permute-start | bytes 5308424 | tf_op jit(solution)/shard_map/ppermute | solution.py:1087
  123.5 1.2 copy-start.12
  128.5 19.9 %collective-permute-start.13 = (bf16[1024,384]{1,0:T(8,128)(2,1)}, bf16[1024,384]{1,0:T(8,128)(2,1)S(1)}, u32[]{:S(2)}, u32[]{:S(2)}) collective-permute-start(bf16[1024,384]{1,0:T(8,128)(2,1)} %get-tuple-element.109.rest_1_), channel_id=1, source_target_pairs={{0,4},{2,6},{4,0},{6,2},{8,12},{10,14},{12,8},{14,10},{16,20},{18,... | collective-permute-start | bytes 2359304 | tf_op jit(solution)/shard_map/ppermute | solution.py:1087
  129.3 17.5 %collective-permute-start.15 = (bf16[896,384]{1,0:T(8,128)(2,1)}, bf16[896,384]{1,0:T(8,128)(2,1)}, u32[]{:S(2)}, u32[]{:S(2)}) collective-permute-start(bf16[896,384]{1,0:T(8,128)(2,1)} %get-tuple-element.112.rest_0_), channel_id=1, source_target_pairs={{0,1},{1,0},{2,3},{3,2},{4,5},{5,4},{6,7},{7,6},{8,9},{9,8},{10,11... | collective-permute-start | bytes 2064392 | tf_op jit(solution)/shard_map/ppermute | solution.py:1089
  129.6 16.8 %collective-permute-start.16 = (bf16[384,384]{1,0:T(8,128)(2,1)}, bf16[384,384]{1,0:T(8,128)(2,1)S(1)}, u32[]{:S(2)}, u32[]{:S(2)}) collective-permute-start(bf16[384,384]{1,0:T(8,128)(2,1)} %get-tuple-element.114.rest_3_), channel_id=1, source_target_pairs={{0,16},{2,18},{4,20},{6,22},{8,24},{10,26},{12,28},{14,30},{16,0},... | collective-permute-start | bytes 884744 | tf_op jit(solution)/shard_map/ppermute | solution.py:1087
  132.2 14.2 %collective-permute-start.17 = (bf16[192,384]{1,0:T(8,128)(2,1)}, bf16[192,384]{1,0:T(8,128)(2,1)S(1)}, u32[]{:S(2)}, u32[]{:S(2)}) collective-permute-start(bf16[192,384]{1,0:T(8,128)(2,1)} %get-tuple-element.113.rest_2_), channel_id=1, source_target_pairs={{0,8},{2,10},{4,12},{6,14},{8,0},{10,2},{12,4},{14,6},{16,24},{18,... | collective-permute-start | bytes 442376 | tf_op jit(solution)/shard_map/ppermute | solution.py:1087
  146.4 4.2 %collective-permute-start.14 = (bf16[672,384]{1,0:T(8,128)(2,1)}, bf16[672,384]{1,0:T(8,128)(2,1)S(1)}, u32[]{:S(2)}, u32[]{:S(2)}) collective-permute-start(bf16[672,384]{1,0:T(8,128)(2,1)} %get-tuple-element.116), channel_id=1, source_target_pairs={{0,2},{2,0},{4,6},{6,4},{8,10},{10,8},{12,14},{14,12},{16,18},{18,... | collective-permute-start | bytes 1548296 | tf_op jit(solution)/shard_map/ppermute | solution.py:1087
  146.5 1.9 copy-start.24
  146.5 1.8 copy-start.20
  148.3 0.9 copy-start.15
  155.1 17.1 %collective-permute-start.18 = (bf16[560,384]{1,0:T(8,128)(2,1)}, bf16[560,384]{1,0:T(8,128)(2,1)S(1)}, u32[]{:S(2)}, u32[]{:S(2)}) collective-permute-start(bf16[560,384]{1,0:T(8,128)(2,1)} %get-tuple-element.118), channel_id=1, source_target_pairs={{0,1},{1,0},{2,3},{3,2},{4,5},{5,4},{6,7},{7,6},{8,9},{9,8},{10,11... | collective-permute-start | bytes 1290248 | tf_op jit(solution)/shard_map/ppermute | solution.py:1089
  155.4 15.9 %collective-permute-start.19 = (bf16[496,384]{1,0:T(8,128)(2,1)}, bf16[496,384]{1,0:T(8,128)(2,1)S(1)}, u32[]{:S(2)}, u32[]{:S(2)}) collective-permute-start(bf16[496,384]{1,0:T(8,128)(2,1)} %get-tuple-element.119), channel_id=1, source_target_pairs={{0,4},{2,6},{4,0},{6,2},{8,12},{10,14},{12,8},{14,10},{16,20},{18,... | collective-permute-start | bytes 1142792 | tf_op jit(solution)/shard_map/ppermute | solution.py:1087
  156.3 14.4 %collective-permute-start.20 = (bf16[240,384]{1,0:T(8,128)(2,1)}, bf16[240,384]{1,0:T(8,128)(2,1)S(1)}, u32[]{:S(2)}, u32[]{:S(2)}) collective-permute-start(bf16[240,384]{1,0:T(8,128)(2,1)} %get-tuple-element.120), channel_id=1, source_target_pairs={{0,5},{1,4},{2,7},{3,6},{4,1},{5,0},{6,3},{7,2},{8,13},{9,12},{10,... | collective-permute-start | bytes 552968 | tf_op jit(solution)/shard_map/ppermute | solution.py:1093
  158.6 4.6 %copy-start.18 = (bf16[2,320,384]{2,1,0:T(8,128)(2,1)S(1)}, bf16[2,320,384]{2,1,0:T(8,128)(2,1)}, u32[]{:S(2)}) copy-start(bf16[2,320,384]{2,1,0:T(8,128)(2,1)} %get-tuple-element.126) | copy-start | bytes 1474564
  163.2 25.9 %collective-permute-start.21 = (bf16[640,384]{1,0:T(8,128)(2,1)S(1)}, bf16[640,384]{1,0:T(8,128)(2,1)S(1)}, u32[]{:S(2)}, u32[]{:S(2)}) collective-permute-start(bf16[640,384]{1,0:T(8,128)(2,1)S(1)} %bitcast.19), channel_id=1, source_target_pairs={{0,1},{1,0},{2,3},{3,2},{4,5},{5,4},{6,7},{7,6},{8,9},{9,8},{10,11... | collective-permute-start | bytes 1474568 | tf_op jit(solution)/shard_map/ppermute | solution.py:1089
  163.6 31.3 %collective-permute-start.25 = (bf16[288,384]{1,0:T(8,128)(2,1)}, bf16[288,384]{1,0:T(8,128)(2,1)}, u32[]{:S(2)}, u32[]{:S(2)}) collective-permute-start(bf16[288,384]{1,0:T(8,128)(2,1)} %get-tuple-element.128), channel_id=1, source_target_pairs={{0,16},{2,18},{4,20},{6,22},{8,24},{10,26},{12,28},{14,30},{16,0},... | collective-permute-start | bytes 663560 | tf_op jit(solution)/shard_map/ppermute | solution.py:1087
  170.7 1.5 copy-start.4
  170.7 24.2 %collective-permute-start.26 = (bf16[192,384]{1,0:T(8,128)(2,1)}, bf16[192,384]{1,0:T(8,128)(2,1)}, u32[]{:S(2)}, u32[]{:S(2)}) collective-permute-start(bf16[192,384]{1,0:T(8,128)(2,1)} %get-tuple-element.129), channel_id=1, source_target_pairs={{0,8},{2,10},{4,12},{6,14},{8,0},{10,2},{12,4},{14,6},{16,24},{18,... | collective-permute-start | bytes 442376 | tf_op jit(solution)/shard_map/ppermute | solution.py:1087
  175.6 19.3 %collective-permute-start.22 = (bf16[480,384]{1,0:T(8,128)(2,1)}, bf16[480,384]{1,0:T(8,128)(2,1)S(1)}, u32[]{:S(2)}, u32[]{:S(2)}) collective-permute-start(bf16[480,384]{1,0:T(8,128)(2,1)} %get-tuple-element.123.rest_0_), channel_id=1, source_target_pairs={{0,8},{2,10},{4,12},{6,14},{8,0},{10,2},{12,4},{14,6},{16,24},{18,... | collective-permute-start | bytes 1105928 | tf_op jit(solution)/shard_map/ppermute | solution.py:1087
  176.3 25.0 %collective-permute-start.23 = (bf16[192,384]{1,0:T(8,128)(2,1)}, bf16[192,384]{1,0:T(8,128)(2,1)S(1)}, u32[]{:S(2)}, u32[]{:S(2)}) collective-permute-start(bf16[192,384]{1,0:T(8,128)(2,1)} %get-tuple-element.124.rest_1_), channel_id=1, source_target_pairs={{0,16},{2,18},{4,20},{6,22},{8,24},{10,26},{12,28},{14,30},{16,0},... | collective-permute-start | bytes 442376 | tf_op jit(solution)/shard_map/ppermute | solution.py:1087
  178.9 10.2 %copy-start.26 = (bf16[192,384]{1,0:T(8,128)(2,1)S(1)}, bf16[192,384]{1,0:T(8,128)(2,1)}, u32[]{:S(2)}) copy-start(bf16[192,384]{1,0:T(8,128)(2,1)} %get-tuple-element.125.rest_2_) | copy-start | bytes 442372
  189.1 1.2 copy-start.19
  189.1 12.2 %collective-permute-start.24 = (bf16[192,384]{1,0:T(8,128)(2,1)S(1)}, bf16[192,384]{1,0:T(8,128)(2,1)S(1)}, u32[]{:S(2)}, u32[]{:S(2)}) collective-permute-start(bf16[192,384]{1,0:T(8,128)(2,1)S(1)} %copy-done.26), channel_id=1, source_target_pairs={{0,24},{2,26},{4,28},{6,30},{8,16},{10,18},{12,20},{14,22},{16,8},... | collective-permute-start | bytes 442376 | tf_op jit(solution)/shard_map/ppermute | solution.py:1087
  198.0 8.7 %collective-permute-start.30 = (bf16[240,384]{1,0:T(8,128)(2,1)}, bf16[240,384]{1,0:T(8,128)(2,1)S(1)}, u32[]{:S(2)}, u32[]{:S(2)}) collective-permute-start(bf16[240,384]{1,0:T(8,128)(2,1)} %get-tuple-element.130.refs_9_), channel_id=1, source_target_pairs={{0,16},{2,18},{4,20},{6,22},{8,24},{10,26},{12,28},{14,30},{16,0},... | collective-permute-start | bytes 552968 | tf_op jit(solution)/shard_map/ppermute | solution.py:1087
  199.8 6.7 %collective-permute-start.31 = (bf16[192,384]{1,0:T(8,128)(2,1)}, bf16[192,384]{1,0:T(8,128)(2,1)S(1)}, u32[]{:S(2)}, u32[]{:S(2)}) collective-permute-start(bf16[192,384]{1,0:T(8,128)(2,1)} %get-tuple-element.131.refs_10_), channel_id=1, source_target_pairs={{0,8},{2,10},{4,12},{6,14},{8,0},{10,2},{12,4},{14,6},{16,24},{18,... | collective-permute-start | bytes 442376 | tf_op jit(solution)/shard_map/ppermute | solution.py:1087
  204.3 6.4 %collective-permute-start.27 = (bf16[160,384]{1,0:T(8,128)(2,1)}, bf16[160,384]{1,0:T(8,128)(2,1)S(1)}, u32[]{:S(2)}, u32[]{:S(2)}) collective-permute-start(bf16[160,384]{1,0:T(8,128)(2,1)} %get-tuple-element.133.own_ref), channel_id=1, source_target_pairs={{0,4},{2,6},{4,0},{6,2},{8,12},{10,14},{12,8},{14,10},{16,20},{18,... | collective-permute-start | bytes 368648 | tf_op jit(solution)/shard_map/ppermute | solution.py:1087
  205.1 5.5 %collective-permute-start.28 = (bf16[160,384]{1,0:T(8,128)(2,1)}, bf16[160,384]{1,0:T(8,128)(2,1)S(1)}, u32[]{:S(2)}, u32[]{:S(2)}) collective-permute-start(bf16[160,384]{1,0:T(8,128)(2,1)} %get-tuple-element.133.own_ref), channel_id=1, source_target_pairs={{0,2},{2,0},{4,6},{6,4},{8,10},{10,8},{12,14},{14,12},{16,18},{18,... | collective-permute-start | bytes 368648 | tf_op jit(solution)/shard_map/ppermute | solution.py:1087
  205.1 5.8 %collective-permute-start.29 = (bf16[160,384]{1,0:T(8,128)(2,1)}, bf16[160,384]{1,0:T(8,128)(2,1)S(1)}, u32[]{:S(2)}, u32[]{:S(2)}) collective-permute-start(bf16[160,384]{1,0:T(8,128)(2,1)} %get-tuple-element.133.own_ref), channel_id=1, source_target_pairs={{0,6},{2,4},{4,2},{6,0},{8,14},{10,12},{12,10},{14,8},{16,22},{18,... | collective-permute-start | bytes 368648 | tf_op jit(solution)/shard_map/ppermute | solution.py:1087
  (14 other events, 10.3 us)
